TPU v7x, 1024 devices: a whole 4x4x32 slice. The times are simulated.
1024 devices in a mesh: exp: 8 (over y, core), et: 128 (over x, z).
Axes of the slice: x: 4, y: 4, z: 32, core: 2. Of those that a mesh axis runs over, the one named last changes fastest.
Arguments:
- grad_out: bfloat16 [1024, 4096], P(('exp', 'et')), may hold values from -3 to 3
- route_weight: bfloat16 [1024, 8], P(('exp', 'et')), may hold values from 0.099609375 to 1
- expert_ids: int32 [1024, 8], P(('exp', 'et')), may hold values from 0 to 63, as said below
- slot_ids: int32 [1024, 8], P(('exp', 'et')), may hold values from 0 to 29, as said below
- saved_pre: bfloat16 [1024, 240, 192], P(('exp', 'et')), may hold values from -6 to 6
- gate_proj: bfloat16 [1024, 96, 4096], P(('exp', 'et')), may hold values from -0.09375 to 0.09375
- up_proj: bfloat16 [1024, 96, 4096], P(('exp', 'et')), may hold values from -0.09375 to 0.09375
- down_proj: bfloat16 [1024, 96, 4096], P(('exp', 'et')), may hold values from -0.15625 to 0.15625
Outputs:
- grad_tokens: bfloat16 [1024, 4096], P(('exp', 'et'))
- grad_weights: float32 [1024, 8], P(('exp', 'et'))
- grad_down: bfloat16 [1024, 96, 4096], P(('exp', 'et'))
Inputs may be any that keep to these rules, and one draw needn't show every extreme that they name: `expert_ids`: each token names 8 different experts. Among the tokens of each aligned block of 128 tokens (one index of exp), every expert is named 2 to 30 times, and one expert, the same in every block, is named exactly 30 times. slot_ids[t, k] is the rank of choice (t, k) among the choices of its block that name the same expert, counted by token and then by choice.
All inputs are finite; a program needn't handle non-finite values.
Results may differ from a plain program's by a relative error of at most 0.02.
Values may be sent and summed in bfloat16 or wider, within the bound.
A program may use at most 64 MiB of HBM per device.

v0:
```python
import jax
import jax.numpy as jnp
from jax import lax
from jax.sharding import PartitionSpec as P

FF = 1536


def partner_2(block, axis, apart):
    count = lax.axis_size(axis)
    route = []
    for low in range(count):
        high = low | 1 << apart
        if high != low and high < count:
            route += [(low, high), (high, low)]
    return lax.ppermute(block, axis, route)


def body(grad_out, route_weight, expert_ids, slot_ids, saved_pre, gate_proj, up_proj, down_proj):
    exp_size = lax.axis_size("exp")
    et_size = lax.axis_size("et")
    et_index = lax.axis_index("et")
    tok_dev, model_width = grad_out.shape
    top_count = expert_ids.shape[1]
    slice_units = gate_proj.shape[1]
    hid_split = FF // slice_units
    exp_row = et_size // hid_split
    slot_count = saved_pre.shape[1]
    capacity = slot_count // exp_size
    row_tokens = et_size * tok_dev
    column = et_index // hid_split
    my_slice = et_index % hid_split
    col_width = model_width // hid_split
    first_col = my_slice * col_width
    rows_buf = jnp.zeros((slot_count, col_width), jnp.bfloat16)
    weight_buf = jnp.zeros((slot_count,), jnp.bfloat16)
    owner_buf = jnp.full((slot_count,), -1, jnp.int32)
    grad_piece = lax.all_gather(grad_out, "et", axis=0, tiled=True)
    weight_piece = lax.all_gather(route_weight, "et", axis=0, tiled=True)
    id_piece = lax.all_gather(expert_ids, "et", axis=0, tiled=True)
    slot_piece = lax.all_gather(slot_ids, "et", axis=0, tiled=True)
    picked = lax.dynamic_slice_in_dim(grad_piece, first_col, col_width, 1)
    positions = jnp.arange(grad_piece.shape[0], dtype=jnp.int32)
    matched = id_piece % exp_row == column
    target = jnp.where(matched, id_piece // exp_row * capacity + slot_piece, exp_size * capacity)
    for slot_k in range(top_count):
        where_to = target[:, slot_k]
        rows_buf = rows_buf.at[where_to].set(picked, mode="drop")
        weight_buf = weight_buf.at[where_to].set(weight_piece[:, slot_k], mode="drop")
        owner_buf = owner_buf.at[where_to].set(positions * top_count + slot_k, mode="drop")
    rows_buf, weight_buf, owner_buf = (rows_buf, weight_buf, owner_buf)
    send_rows = rows_buf.reshape(exp_size, capacity, col_width)
    send_weight = weight_buf.reshape(exp_size, capacity)
    got_rows, got_weight = (
        lax.all_to_all(send_rows, "exp", split_axis=0, concat_axis=0, tiled=True),
        lax.all_to_all(send_weight, "exp", split_axis=0, concat_axis=0, tiled=True),
    )
    for bit_pos in range(hid_split.bit_length() - 1):
        partner = partner_2(got_rows, "et", bit_pos)
        upper_half = et_index // (1 << bit_pos) % 2
        got_rows = jnp.where(
            upper_half == 1,
            jnp.concatenate([partner, got_rows], axis=2),
            jnp.concatenate([got_rows, partner], axis=2),
        )
    slot_rows = got_rows.reshape(slot_count, model_width)
    slot_weight = got_weight.reshape(slot_count).astype(jnp.float32)[:, None]
    pre_local = saved_pre[0]
    gate_pre = pre_local[:, :slice_units].astype(jnp.float32)
    up_pre = pre_local[:, slice_units:].astype(jnp.float32)
    sigmoid_gate = jax.nn.sigmoid(gate_pre)
    active = gate_pre * sigmoid_gate
    product = active * up_pre
    hidden = product.astype(jnp.bfloat16)
    weighted = (slot_weight * product).astype(jnp.bfloat16)
    back_proj = jnp.einsum("sd,fd->sf", slot_rows, down_proj[0], preferred_element_type=jnp.float32)
    scaled = slot_weight * back_proj
    grad_gate = (scaled * up_pre * sigmoid_gate * (1.0 + gate_pre * (1.0 - sigmoid_gate))).astype(
        jnp.bfloat16
    )
    grad_up = (scaled * active).astype(jnp.bfloat16)
    part_grad = (
        jnp.dot(grad_gate, gate_proj[0], preferred_element_type=jnp.float32)
        + jnp.dot(grad_up, up_proj[0], preferred_element_type=jnp.float32)
    ).astype(jnp.bfloat16)
    output_rows = jnp.dot(hidden, down_proj[0], preferred_element_type=jnp.float32)
    part_prob = jnp.sum(slot_rows.astype(jnp.float32) * output_rows, axis=1)
    part_prob = part_prob.astype(jnp.bfloat16)
    down_grad = jnp.einsum(
        "sf,sd->fd", weighted, slot_rows, preferred_element_type=jnp.float32
    ).astype(jnp.bfloat16)[None]
    back_rows, back_prob = (
        lax.all_to_all(
            part_grad.reshape(exp_size, capacity, model_width),
            "exp",
            split_axis=0,
            concat_axis=0,
            tiled=True,
        ),
        lax.all_to_all(
            part_prob.reshape(exp_size, capacity), "exp", split_axis=0, concat_axis=0, tiled=True
        ),
    )
    is_owned = owner_buf >= 0
    token_slot = jnp.where(is_owned, owner_buf // top_count, row_tokens)
    route_slot = jnp.where(is_owned, owner_buf, row_tokens * top_count)
    dense_grad = (
        jnp.zeros((row_tokens, model_width), jnp.float32)
        .at[token_slot]
        .add(back_rows.reshape(slot_count, model_width).astype(jnp.float32), mode="drop")
    )
    dense_prob = (
        jnp.zeros((row_tokens * top_count,), jnp.float32)
        .at[route_slot]
        .add(back_prob.reshape(slot_count).astype(jnp.float32), mode="drop")
        .reshape(row_tokens, top_count)
    )
    summed_grad, summed_prob = (
        lax.psum_scatter(dense_grad, "et", scatter_dimension=0, tiled=True),
        lax.psum_scatter(dense_prob, "et", scatter_dimension=0, tiled=True),
    )
    return (summed_grad.astype(jnp.bfloat16), summed_prob, down_grad)


def solution(mesh):
    in_specs = (
        P(("exp", "et"), None),
        P(("exp", "et"), None),
        P(("exp", "et"), None),
        P(("exp", "et"), None),
        P(("exp", "et"), None, None),
        P(("exp", "et"), None, None),
        P(("exp", "et"), None, None),
        P(("exp", "et"), None, None),
    )
    out_specs = (P(("exp", "et"), None), P(("exp", "et"), None), P(("exp", "et"), None, None))
    return jax.shard_map(body, mesh=mesh, in_specs=in_specs, out_specs=out_specs, check_vma=False)
```

profile of v0, /device:TPU:8, one launch (start us, length us, event | category | flops | bytes accessed | tf_op | source)
XLA Modules:
  0.0 1368.8 jit_solution(6945923859613980055)
XLA Ops:
  7.2 0.7 all-gather.6.cloned.1.call-update
  7.9 157.1 %all-gather = s32[128,1,8]{2,1,0:T(1,128)S(1)} all-gather(s32[1,1,8]{2,1,0:T(1,128)} %bitcast.80), channel_id=1, replica_groups=mesh['exp'=8,'et'=128] {'et'}, dimensions={0}, use_global_device_ids=true | all-gather | bytes 4128 | tf_op jit(solution)/shard_map/all_gather | solution.py:40
  165.1 142.3 %all-gather.1 = s32[128,1,8]{2,1,0:T(1,128)S(1)} all-gather(s32[1,1,8]{2,1,0:T(1,128)} %bitcast.81), channel_id=1, replica_groups=mesh['exp'=8,'et'=128] {'et'}, dimensions={0}, use_global_device_ids=true | all-gather | bytes 4128 | tf_op jit(solution)/shard_map/all_gather | solution.py:41
  307.8 1.0 constant_dynamic-slice_fusion.1
  308.9 1.1 scatter_custom_fusion.16
  309.9 1.1 scatter_custom_fusion.17
  311.0 1.1 scatter_custom_fusion.18
  312.1 1.1 scatter_custom_fusion.19
  313.3 1.1 scatter_custom_fusion.20
  314.4 1.1 scatter_custom_fusion.21
  315.5 1.1 scatter_custom_fusion.22
  316.6 1.1 scatter_custom_fusion.23
  317.8 9.4 all_to_all.26
  327.1 2.4 collective-permute-start
  329.5 4.6 collective-permute-done
  334.2 3.7 collective-permute-start.1
  337.9 11.5 collective-permute-done.1
  349.6 6.0 collective-permute-start.2
  355.6 44.5 %collective-permute-done.2 = bf16[8,30,1024]{2,1,0:T(8,128)(2,1)S(1)} collective-permute-done((bf16[8,30,1024]{2,1,0:T(8,128)(2,1)S(1)}, bf16[8,30,1024]{2,1,0:T(8,128)(2,1)S(1)}, u32[]{:S(2)}, u32[]{:S(2)}) %collective-permute-start.2) | collective-permute-done | bytes 491552 | tf_op jit(solution)/shard_map/ppermute | solution.py:16
  400.5 0.5 copy.22
  401.1 52.3 %collective-permute-start.3 = (bf16[8,30,2048]{2,0,1:T(8,128)(2,1)S(1)}, bf16[8,30,2048]{2,0,1:T(8,128)(2,1)}, u32[]{:S(2)}, u32[]{:S(2)}) collective-permute-start(bf16[8,30,2048]{2,0,1:T(8,128)(2,1)S(1)} %copy.22), channel_id=1, source_target_pairs={{0,8},{8,0},{1,9},{9,1},{2,10},{10,2},{3,11},{11,3},{4,12},{12,4},... | collective-permute-start | bytes 2949128 | tf_op jit(solution)/shard_map/ppermute | solution.py:16
  453.3 252.9 %all-gather.2 = bf16[128,1,8]{2,1,0:T(2,128)(2,1)S(1)} all-gather(bf16[1,1,8]{2,1,0:T(2,128)(2,1)S(1)} %bitcast.82), channel_id=1, replica_groups=mesh['exp'=8,'et'=128] {'et'}, dimensions={0}, use_global_device_ids=true | all-gather | bytes 2064 | tf_op jit(solution)/shard_map/all_gather | solution.py:39
  706.3 1.3 scatter_custom_fusion.8
  707.6 1.3 scatter_fusion.7
  709.0 1.5 scatter_fusion.8
  710.5 1.3 scatter_fusion.9
  711.9 1.3 scatter_fusion.10
  713.2 1.3 scatter_fusion.11
  714.6 1.3 scatter_fusion.12
  716.0 1.3 scatter_fusion.13
  717.3 0.7 all_to_all.21
  718.0 4.7 all-to-all-start
  722.7 3.8 all-to-all-done
  726.7 0.8 concatenate.62
  727.5 1.2 maximum_select_fusion.4
  728.9 1.3 maximum_select_fusion.2
  730.2 1.8 copy.23
  732.0 1.2 concatenate.60
  733.3 2.7 fusion.2
  736.0 0.7 convert_element_type.87
  736.7 4.7 all-to-all-start.3
  741.3 1.9 convolution_multiply_fusion.1
  743.3 0.7 fusion.6
  744.0 0.4 copy-done.3
  744.4 0.7 fusion
  745.1 1.6 reshape.68
  746.8 4.8 all-to-all-start.2
  751.6 1.0 scatter_custom_fusion
  752.6 1.3 dynamic-slice.1
  753.9 1.0 scatter_fusion
  754.9 1.0 scatter_fusion.1
  755.9 1.0 scatter_fusion.2
  756.9 1.2 scatter_fusion.3
  758.1 1.0 scatter_fusion.4
  759.1 1.0 scatter_fusion.5
  760.1 1.0 scatter_fusion.6
  761.1 3.7 fusion.1
  764.9 2.0 scatter_custom_fusion.25
  767.0 10.3 all-to-all-done.2
  777.3 2.1 reshape.269
  779.4 7.6 scatter_custom_fusion.24
  787.0 571.6 %all-reduce.4 = (bf16[128,4096]{1,0:T(8,128)(2,1)}, f32[128,8]{1,0:T(8,128)S(1)}) all-reduce(f32[128,4096]{1,0:T(8,128)S(1)} %scatter_custom_fusion.24, f32[128,8]{1,0:T(8,128)S(1)} %reshape.69), channel_id=2, replica_groups=mesh['exp'=8,'et'=128] {'et'}, use_global_device_ids=true, to_apply=%region_25.26.clone | all-reduce | flops 525312 | bytes 3153920
  1358.7 2.1 dynamic-slice_convert_fusion
  1360.8 1.1 constant_dynamic-slice_fusion
  (41 shorter events, 2.0 us)
Async XLA Ops:
  7.2 736.1 %copy-start = (bf16[1,96,4096]{2,1,0:T(8,128)(2,1)S(1)}, bf16[1,96,4096]{2,1,0:T(8,128)(2,1)}, u32[]{:S(2)}) copy-start(bf16[1,96,4096]{2,1,0:T(8,128)(2,1)} %param.13) | copy-start | bytes 2359300
  7.2 300.6 %all-gather.6.cloned.1.call-start = ((), (), s32[]{:S(2)}) async-start(), calls=%async_computation.4 | async-start | bytes 2113536 | tf_op jit(solution)/shard_map/all_gather | solution.py:38
  327.1 6.9 collective-permute-start
  334.2 15.3 %collective-permute-start.1 = (bf16[8,30,512]{2,1,0:T(8,128)(2,1)S(1)}, bf16[8,30,512]{2,1,0:T(8,128)(2,1)S(1)}, u32[]{:S(2)}, u32[]{:S(2)}) collective-permute-start(bf16[8,30,512]{2,1,0:T(8,128)(2,1)S(1)} %maximum_select_fusion.5), channel_id=1, source_target_pairs={{0,2},{2,0},{1,3},{3,1},{4,6},{6,4},{5,7},{7,5},{8,10},{10,8},{9,1... | collective-permute-start | bytes 737288 | tf_op jit(solution)/shard_map/ppermute | solution.py:16
  349.6 103.7 %copy-start.5 = (bf16[1,8]{1,0:T(2,128)(2,1)S(1)}, bf16[1,8]{1,0:T(2,128)(2,1)}, u32[]{:S(2)}) copy-start(bf16[1,8]{1,0:T(2,128)(2,1)} %param.9) | copy-start | bytes 52
  349.6 50.5 %collective-permute-start.2 = (bf16[8,30,1024]{2,1,0:T(8,128)(2,1)S(1)}, bf16[8,30,1024]{2,1,0:T(8,128)(2,1)S(1)}, u32[]{:S(2)}, u32[]{:S(2)}) collective-permute-start(bf16[8,30,1024]{2,1,0:T(8,128)(2,1)S(1)} %maximum_select_fusion.3), channel_id=1, source_target_pairs={{0,4},{4,0},{1,5},{5,1},{2,6},{6,2},{3,7},{7,3},{8,12},{12,8},{9,1... | collective-permute-start | bytes 1474568 | tf_op jit(solution)/shard_map/ppermute | solution.py:16
  401.1 329.1 %collective-permute-start.3 = (bf16[8,30,2048]{2,0,1:T(8,128)(2,1)S(1)}, bf16[8,30,2048]{2,0,1:T(8,128)(2,1)}, u32[]{:S(2)}, u32[]{:S(2)}) collective-permute-start(bf16[8,30,2048]{2,0,1:T(8,128)(2,1)S(1)} %copy.22), channel_id=1, source_target_pairs={{0,8},{8,0},{1,9},{9,1},{2,10},{10,2},{3,11},{11,3},{4,12},{12,4},... | collective-permute-start | bytes 2949128 | tf_op jit(solution)/shard_map/ppermute | solution.py:16
  718.0 8.4 all-to-all-start
  730.2 3.1 copy-start.1
  730.2 3.1 copy-start.4
  733.3 8.1 copy-start.2
  736.7 10.1 all-to-all-start.3
  743.2 1.1 copy-start.3
  746.8 30.6 %all-to-all-start.2 = ((bf16[8,30,4096]{2,1,0:T(8,128)(2,1)}), bf16[8,30,4096]{2,1,0:T(8,128)(2,1)S(1)}, u32[]{:S(2)}, u32[]{:S(2)}) async-start(bf16[8,30,4096]{2,1,0:T(8,128)(2,1)} %reshape.68), calls=%async_computation.2 | async-start | bytes 4194304 | tf_op jit(solution)/shard_map/all_to_all | solution.py:93
Sparse Core Ops, SparseCore 0:
  12.1 274.2 all-gather.5
where the time goes:
time: 1370 us
  blocking collectives  1130 us (82%)
  starting transfers between devices  78.5 us (6%)
  waiting for transfers between devices  75.3 us (5%)
  local copies, waits for them, and re-layouts  43.9 us (3%)
  between operations  14.6 us (1%)
    unnamed x1, blocking collectives  572 us
    all_gather x1, blocking collectives, body(): weight_piece = lax.all_gather(route_weight, 'et', axis=0, tiled=True)  253 us
    all_gather x1, blocking collectives, body(): id_piece = lax.all_gather(expert_ids, 'et', axis=0, tiled=True)  157 us
    all_gather x1, blocking collectives, body(): slot_piece = lax.all_gather(slot_ids, 'et', axis=0, tiled=True)  142 us
    ppermute x4, starting transfers between devices, partner_2(): return lax.ppermute(block, axis, route)  64.3 us
    ppermute x4, waiting for transfers between devices, partner_2(): return lax.ppermute(block, axis, route)  60.6 us
  transfers between devices with their start and end apart: 8, of which 5 were waited for; matrix products, arithmetic and copies ran while one was open for 3% of the time, Pallas kernels for 0%

commit v1 on v0

v1 whole, which is shorter than its diff:
```python
import jax
import jax.numpy as jnp
from jax import lax
from jax.experimental import pallas as pl
from jax.experimental.pallas import tpu as pltpu
from jax.sharding import PartitionSpec as P

MESH = pl.DeviceIdType.MESH
BF, F32 = jnp.bfloat16, jnp.float32
D, UNITS, TOPK, CAP = 4096, 96, 8, 30
SLOTS, PAD, BLOCKS = 240, 32, 8
ROWS = BLOCKS * PAD
EXT = 128
NX, NZ, NQ = 4, 32, 8
CHUNK = 1024
NCH = D // CHUNK
CUTS = [(0, EXT + CHUNK)] + [(EXT + f * CHUNK, CHUNK) for f in range(1, NCH)]
EXP_STEPS = [(dy, dc) for dy in (1, 3, 2, 0) for dc in (0, 1) if (dy, dc) != (0, 0)]


def dot(a, b, dims=((1,), (0,))):
    return lax.dot_general(a, b, (dims, ((), ())), preferred_element_type=F32)


def kernel(pay, pre, gate_hbm, up_hbm, down_hbm, tok_out, prob_out, down_out,
           abuf, bbuf, frows, g, st, s, ysend, yrecv, psend, precv, xsend, xrecv, acc,
           bsend, brecv, cbuf, arecv, arecv2, wgu, wdn,
           load_sem, a_s, a_r, b_s, b_r, x_s, x_r, y_s, y_r, p_s, p_r, u_s, u_r, v_s, v_r, w_s, w_r):
    ex, et = lax.axis_index("exp"), lax.axis_index("et")
    y, core = ex // 2, ex % 2
    x, z = et // NZ, et % NZ
    q = z // 4
    column = x * 2 + z // 16
    expert = ex * 8 + column

    def at_z(dz):
        return (ex, x * NZ + lax.rem(z + dz + NZ, NZ))

    def at_x(dx):
        return (ex, lax.rem(x + dx, NX) * NZ + z)

    def exp_of(step):
        dy, dc = step
        return lax.rem(y + dy, 4) * 2 + lax.rem(core + dc, 2)

    def slot(j):
        return lax.rem(q + j + NQ, NQ)

    def send(src, dst, ss, rs, device):
        copy = pltpu.make_async_remote_copy(
            src_ref=src, dst_ref=dst, send_sem=ss, recv_sem=rs, device_id=device, device_id_type=MESH)
        copy.start()
        return copy

    sent = []

    loads = [
        pltpu.make_async_copy(gate_hbm.at[0], wgu.at[pl.ds(0, UNITS)], load_sem.at[0]),
        pltpu.make_async_copy(up_hbm.at[0], wgu.at[pl.ds(128, UNITS)], load_sem.at[1]),
        pltpu.make_async_copy(down_hbm.at[0], wdn.at[pl.ds(0, UNITS)], load_sem.at[2]),
    ]
    for load in loads:
        load.start()

    barrier = pltpu.get_barrier_semaphore()
    partners = [at_z(d) for d in (1, -1, 2, -2, 4, -4, 8, -8)]
    partners += [at_x(d) for d in (1, 2, 3)]
    partners += [(exp_of(step), et) for step in EXP_STEPS]
    for device in partners:
        pl.semaphore_signal(barrier, inc=1, device_id=device, device_id_type=MESH)
    abuf[:, pl.ds(q, 1)] = pay[...].reshape(3, 1, 16, 128)
    pad = jnp.zeros((32, D), BF)
    wgu[pl.ds(UNITS, 32)] = pad
    wgu[pl.ds(128 + UNITS, 32)] = pad
    wdn[pl.ds(UNITS, 32)] = pad
    pl.semaphore_wait(barrier, len(partners))

    mine = abuf.at[:, pl.ds(q, 1)]
    first = [send(mine, mine, a_s.at[i], a_r.at[i], at_z(d)) for i, d in enumerate((4, -4, 8, -8))]
    for copy in first:
        copy.wait_recv()
    second = []
    for i, (j, d) in enumerate(((1, -8), (2, -8), (-1, 8))):
        part = abuf.at[:, pl.ds(slot(j), 1)]
        second.append(send(part, part, a_s.at[4 + i], a_r.at[4 + i], at_z(d)))
    for copy in second:
        copy.wait_recv()
    sent += first + second

    bbuf[0, 0:8] = abuf[0]
    bbuf[0, 8] = jnp.sum(abuf[2].astype(F32), axis=0).astype(BF)
    bbuf[0, 9:17] = abuf[1]
    low, high = pl.ds(0, 9), pl.ds(9, 8)
    near = [
        send(bbuf.at[0], bbuf.at[1], b_s.at[0], b_r.at[0], at_z(-1)),
        send(bbuf.at[0], bbuf.at[3], b_s.at[1], b_r.at[1], at_z(1)),
        send(bbuf.at[0, low], bbuf.at[2, low], b_s.at[2], b_r.at[2], at_z(-2)),
        send(bbuf.at[0, high], bbuf.at[2, high], b_s.at[3], b_r.at[3], at_z(2)),
    ]
    for copy in near:
        copy.wait_recv()
    sent += near

    for d in range(4):
        g[d * 8:d * 8 + 8, 0:EXT] = bbuf[d, 8, 0:8]
        for h in range(2):
            frows[(d * 2 + h) * 128:(d * 2 + h + 1) * 128] = (
                bbuf[d, h * 9:h * 9 + 8].astype(F32).reshape(128, 128))
    gathers = []
    for f, (start, width) in enumerate(CUTS):
        h = f // 2
        for i in range((f % 2) * 8, (f % 2) * 8 + 8):
            row = jnp.concatenate(
                [frows[pl.ds((d * 2 + h) * 128 + i, 8, stride=16), :] for d in range(4)], axis=0)
            col = EXT + (h * 16 + i) * 128
            g[0:32, col:col + 128] = row.astype(BF)
        cols = pl.ds(start, width)
        gathers.append([
            send(g.at[pl.ds(0, 32), cols], g.at[pl.ds((4 - dx) * 32, 32), cols],
                 x_s.at[dx - 1, f], x_r.at[dx - 1, f], at_x(dx))
            for dx in (1, 2, 3)])

    mine_rows = pl.ds(pl.multiple_of(ex * PAD, PAD), PAD)
    dispatch = []
    for f, (start, width) in enumerate(CUTS):
        cols = pl.ds(start, width)
        for copy in gathers[f]:
            copy.wait_recv()
        if f == 0:
            ext = g[:, 0:EXT].astype(F32)
            code = ext * 32.0 + pltpu.roll(ext, EXT - TOPK, 1)
            lane = lax.broadcasted_iota(jnp.int32, (128, ROWS), 1)
            target = ((lane // PAD) * 256 + lane % PAD + column * PAD).astype(F32)
            hit = jnp.zeros((128, ROWS), F32)
            for k in range(TOPK):
                hit = hit + jnp.where(code[:, k:k + 1] == target, 1.0, 0.0)
            st[...] = hit.astype(BF)
            s[...] = jnp.transpose(hit).astype(BF)
        ysend[:, start:start + width] = dot(s[...], g[:, start:start + width]).astype(BF)
        copies = []
        for j, step in enumerate(EXP_STEPS):
            to = exp_of(step)
            rows = pl.ds(pl.multiple_of(to * PAD, PAD), PAD)
            copies.append(send(ysend.at[rows, cols], yrecv.at[mine_rows, cols],
                               y_s.at[j, f], y_r.at[j, f], (to, et)))
        yrecv[mine_rows, start:start + width] = ysend[mine_rows, start:start + width]
        dispatch.append(copies)

    for load in loads:
        load.wait()
    slot_row = lax.broadcasted_iota(jnp.int32, (ROWS, SLOTS), 0)
    slot_col = lax.broadcasted_iota(jnp.int32, (ROWS, SLOTS), 1)
    place = (slot_row // PAD) * CAP + slot_row % PAD
    spread = jnp.where((place == slot_col) & (slot_row % PAD < CAP), 1.0, 0.0).astype(BF)
    pre_rows = dot(spread, pre[...]).astype(BF)
    unit_row = lax.broadcasted_iota(jnp.int32, (2 * UNITS, 128), 0)
    unit_col = lax.broadcasted_iota(jnp.int32, (2 * UNITS, 128), 1)
    pick_gate = jnp.where((unit_row == unit_col) & (unit_col < UNITS), 1.0, 0.0).astype(BF)
    pick_up = jnp.where((unit_row == unit_col + UNITS) & (unit_col < UNITS), 1.0, 0.0).astype(BF)
    gate_pre = dot(pre_rows, pick_gate)
    up_pre = dot(pre_rows, pick_up)
    sig = jax.nn.sigmoid(gate_pre)
    active = gate_pre * sig
    product = active * up_pre
    hidden = product.astype(BF).astype(F32)
    gate_factor = up_pre * sig * (1.0 + gate_pre * (1.0 - sig))

    back = jnp.zeros((ROWS, 128), F32)
    for f, (start, width) in enumerate(CUTS):
        for copy in dispatch[f]:
            copy.wait_recv()
        back = back + dot(yrecv[:, EXT + f * CHUNK:EXT + (f + 1) * CHUNK],
                          wdn[:, f * CHUNK:(f + 1) * CHUNK], ((1,), (1,)))
        sent += dispatch[f] + gathers[f]

    ext = yrecv[:, 0:EXT].astype(F32)
    lane = lax.broadcasted_iota(jnp.int32, (ROWS, EXT), 1)
    named = (lane < TOPK) & (ext.astype(jnp.int32) == expert)
    weight = jnp.sum(jnp.where(named, pltpu.roll(ext, EXT - 2 * TOPK, 1), 0.0), axis=1, keepdims=True)
    scaled = weight * back
    grads = jnp.concatenate([scaled * gate_factor, scaled * active], axis=1).astype(BF)
    part_prob = jnp.sum(hidden * back, axis=1, keepdims=True)
    psend[:, 0:EXT] = jnp.where(named, part_prob, 0.0).astype(BF)
    weighted = jnp.transpose(weight * product).astype(BF)

    combine = []
    for f, (start, width) in enumerate(CUTS):
        cols = pl.ds(start, width)
        psend[:, EXT + f * CHUNK:EXT + (f + 1) * CHUNK] = dot(
            grads, wgu[:, f * CHUNK:(f + 1) * CHUNK]).astype(BF)
        copies = []
        for j, step in enumerate(EXP_STEPS):
            to = exp_of(step)
            rows = pl.ds(pl.multiple_of(to * PAD, PAD), PAD)
            copies.append(send(psend.at[rows, cols], precv.at[mine_rows, cols],
                               p_s.at[j, f], p_r.at[j, f], (to, et)))
        precv[mine_rows, start:start + width] = psend[mine_rows, start:start + width]
        combine.append(copies)

    for f in range(NCH):
        down_out[:, f * CHUNK:(f + 1) * CHUNK] = dot(
            weighted, yrecv[:, EXT + f * CHUNK:EXT + (f + 1) * CHUNK])[0:UNITS].astype(BF)

    reduces = []
    for f, (start, width) in enumerate(CUTS):
        cols = pl.ds(start, width)
        for copy in combine[f]:
            copy.wait_recv()
        sent += combine[f]
        dense = dot(st[...], precv[:, start:start + width])
        acc[:, start:start + width] = dense[0:32]
        xsend[:, start:start + width] = dense[32:128].astype(BF)
        reduces.append([
            send(xsend.at[pl.ds((dx - 1) * 32, 32), cols], xrecv.at[dx - 1, :, cols],
                 u_s.at[dx - 1, f], u_r.at[dx - 1, f], at_x(dx))
            for dx in (1, 2, 3)])
    for f, (start, width) in enumerate(CUTS):
        for copy in reduces[f]:
            copy.wait_recv()
        sent += reduces[f]
        total = acc[:, start:start + width]
        for i in range(3):
            total = total + xrecv[i, :, start:start + width].astype(F32)
        if f == 0:
            ext_total = total[:, 0:EXT]
            total = total[:, EXT:]
        h = f // 2
        for i in range(8):
            for d in range(4):
                frows[pl.ds((d * 2 + h) * 128 + (f % 2) * 8 + i, 8, stride=16), :] = (
                    total[d * 8:d * 8 + 8, i * 128:(i + 1) * 128])

    for d in range(1, 4):
        for h in range(2):
            bsend[d - 1, h * 9:h * 9 + 8] = (
                frows[(d * 2 + h) * 128:(d * 2 + h + 1) * 128].reshape(8, 16, 128).astype(BF))
        bsend[d - 1, 8] = jnp.concatenate(
            [ext_total[d * 8:d * 8 + 8], jnp.zeros((8, 128), F32)], axis=0).astype(BF)
    near = [
        send(bsend.at[0], brecv.at[0], v_s.at[0], v_r.at[0], at_z(1)),
        send(bsend.at[2], brecv.at[1], v_s.at[1], v_r.at[1], at_z(-1)),
        send(bsend.at[1, low], brecv.at[2, low], v_s.at[2], v_r.at[2], at_z(2)),
        send(bsend.at[1, high], brecv.at[2, high], v_s.at[3], v_r.at[3], at_z(-2)),
    ]
    for copy in near:
        copy.wait_recv()
    sent += near
    for h in range(2):
        total = frows[h * 128:(h + 1) * 128].reshape(8, 16, 128)
        for i in range(3):
            total = total + brecv[i, h * 9:h * 9 + 8].astype(F32)
        cbuf[h] = total
    total = jnp.concatenate([ext_total[0:8], jnp.zeros((8, 128), F32)], axis=0)
    for i in range(3):
        total = total + brecv[i, 8].astype(F32)
    for j in range(8):
        cbuf[2, j] = total

    for j in range(8):
        arecv2[:, j] = cbuf[:, j].astype(BF)
    third = []
    for i, (j, d) in enumerate(((3, 8), (4, 8), (-3, -8))):
        third.append(send(arecv2.at[:, pl.ds(slot(j), 1)], arecv.at[i], w_s.at[i], w_r.at[i], at_z(d)))
    for copy in third:
        copy.wait_recv()
    for i, j in enumerate((1, 2, -1)):
        part = cbuf[:, pl.ds(slot(j), 1)] + arecv[i].astype(F32)
        arecv2[:, pl.ds(slot(j), 1)] = part.astype(BF)
    fourth = []
    for i, (j, d) in enumerate(((1, 4), (-1, -4), (2, 8), (-2, -8))):
        fourth.append(send(arecv2.at[:, pl.ds(slot(j), 1)], arecv.at[3 + i],
                           w_s.at[3 + i], w_r.at[3 + i], at_z(d)))
    for copy in fourth:
        copy.wait_recv()
    sent += third + fourth
    total = cbuf[:, pl.ds(q, 1)]
    for i in range(4):
        total = total + arecv[3 + i].astype(F32)
    total = total.reshape(3, 16, 128)
    tok_out[...] = total[0:2].astype(BF)
    prob_out[...] = total[2]
    for copy in sent:
        copy.wait_send()


def body(grad_out, route_weight, expert_ids, slot_ids, saved_pre, gate_proj, up_proj, down_proj):
    q = lax.axis_index("et") % NZ // 4
    extra = jnp.concatenate(
        [expert_ids.astype(BF), slot_ids.astype(BF), route_weight, jnp.zeros((1, EXT - 3 * TOPK), BF)], axis=1)
    extra = jnp.where(jnp.arange(16)[:, None] == q, extra, jnp.zeros((), BF))
    pay = jnp.concatenate([grad_out.reshape(2, 16, 128), extra[None]], axis=0)
    vmem = pl.BlockSpec(memory_space=pltpu.VMEM)
    hbm = pl.BlockSpec(memory_space=pl.ANY)
    wide = EXT + D
    dma = lambda *shape: pltpu.SemaphoreType.DMA(shape)
    tokens, probs, down_grad = pl.pallas_call(
        kernel,
        out_shape=(
            jax.ShapeDtypeStruct((2, 16, 128), BF),
            jax.ShapeDtypeStruct((16, 128), F32),
            jax.ShapeDtypeStruct((UNITS, D), BF),
        ),
        in_specs=[vmem, vmem, hbm, hbm, hbm],
        out_specs=(vmem, vmem, vmem),
        scratch_shapes=[
            pltpu.VMEM((3, 8, 16, 128), BF),
            pltpu.VMEM((4, 17, 16, 128), BF),
            pltpu.VMEM((1024, 128), F32),
            pltpu.VMEM((128, wide), BF),
            pltpu.VMEM((128, ROWS), BF),
            pltpu.VMEM((ROWS, 128), BF),
            pltpu.VMEM((ROWS, wide), BF),
            pltpu.VMEM((ROWS, wide), BF),
            pltpu.VMEM((ROWS, wide), BF),
            pltpu.VMEM((ROWS, wide), BF),
            pltpu.VMEM((96, wide), BF),
            pltpu.VMEM((3, 32, wide), BF),
            pltpu.VMEM((32, wide), F32),
            pltpu.VMEM((3, 17, 16, 128), BF),
            pltpu.VMEM((3, 17, 16, 128), BF),
            pltpu.VMEM((3, 8, 16, 128), F32),
            pltpu.VMEM((7, 3, 1, 16, 128), BF),
            pltpu.VMEM((3, 8, 16, 128), BF),
            pltpu.VMEM((256, D), BF),
            pltpu.VMEM((128, D), BF),
            dma(3), dma(7), dma(7), dma(4), dma(4), dma(3, NCH), dma(3, NCH), dma(7, NCH), dma(7, NCH),
            dma(7, NCH), dma(7, NCH), dma(3, NCH), dma(3, NCH), dma(4), dma(4), dma(7), dma(7),
        ],
        compiler_params=pltpu.CompilerParams(
            collective_id=0, has_side_effects=True, vmem_limit_bytes=50 * 2**20),
    )(pay, saved_pre[0], gate_proj, up_proj, down_proj)
    return tokens.reshape(1, D), lax.dynamic_slice(probs, (q, 0), (1, TOPK)), down_grad[None]


def solution(mesh):
    rows, blocks = P(("exp", "et"), None), P(("exp", "et"), None, None)
    return jax.shard_map(
        body, mesh=mesh, in_specs=(rows, rows, rows, rows, blocks, blocks, blocks, blocks),
        out_specs=(rows, rows, blocks), check_vma=False)
```

time: 1370 us -> 136 us (0.10)
  the two profiles are of different devices: /device:TPU:8 before, /device:TPU:6 now
where the time goes in v1:
time: 136 us; the launch traced here: 135 us
  Pallas kernels  126 us (93%)
  local copies, waits for them, and re-layouts  5.52 us (4%)
  other arithmetic  2.91 us (2%)
    pallas_call x1, Pallas kernels, body(): pl.pallas_call(kernel, out_shape=(jax.ShapeDtypeStruct((2, 16, 128), BF),...  126 us
    unnamed x10, local copies, waits for them, and re-layouts  4.38 us

profile of v1, /device:TPU:6, one launch (start us, length us, event | category | flops | bytes accessed | tf_op | source)
XLA Modules:
  0.0 134.7 jit_solution(12869477591988536936)
XLA Ops:
  0.6 0.0 copy-start.3
  0.7 0.7 convert_element_type.6
  1.4 0.7 convert_element_type.7
  2.0 0.7 fusion
  2.7 0.1 broadcast_select_fusion
  2.8 0.8 reduce
  3.6 0.0 copy-done.3
  3.6 0.1 copy.11
  3.7 0.0 copy-start
  3.7 1.1 copy-done
  4.9 0.0 copy-start.1
  4.9 1.1 copy-done.1
  6.0 0.0 copy-start.2
  6.0 1.1 copy-done.2
  7.1 125.6 %shard_map.103 = (bf16[2,16,128]{2,1,0:T(8,128)(2,1)S(1)}, f32[16,128]{1,0:T(8,128)S(1)}, bf16[96,4096]{1,0:T(8,128)(2,1)S(1)}) custom-call(bf16[3,16,128]{2,1,0:T(8,128)(2,1)S(1)} %pad_maximum_fusion.pay, bf16[240,192]{1,0:T(8,128)(2,1)S(1)} %bitcast.10, bf16[1,96,4096]{2,1,0:T(8,128)(2,1)S(1)} %copy-done, bf16[1,96,4096]{2,1,0:T(8,128)(2,1)S(1)} %copy-done.1, ...), custom_call_target="tpu_custom_call" | custom-call | tf_op jit(solution)/shard_map/pallas_call | solution.py:296
  132.7 0.5 constant_dynamic-slice_fusion
  133.2 0.6 reshape.64
  133.8 0.9 copy.13
  (3 shorter events, 0.0 us)
Async XLA Ops:
  0.6 3.0 %copy-start.3 = (bf16[1,240,192]{1,2,0:T(8,128)(2,1)S(1)}, bf16[1,240,192]{1,2,0:T(8,128)(2,1)}, u32[]{:S(2)}) copy-start(bf16[1,240,192]{1,2,0:T(8,128)(2,1)} %param.12) | copy-start | bytes 276484
  3.7 1.1 copy-start
  4.9 1.1 copy-start.1
  6.0 1.1 copy-start.2

commit v2 on v1

--- a/solution.py
+++ b/solution.py
@@ -12,9 +12,19 @@
 ROWS = BLOCKS * PAD
 EXT = 128
 NX, NZ, NQ = 4, 32, 8
-CHUNK = 1024
-NCH = D // CHUNK
-CUTS = [(0, EXT + CHUNK)] + [(EXT + f * CHUNK, CHUNK) for f in range(1, NCH)]
+OWN, BOTH = 8, 16
+WO, WB = OWN * 128, BOTH * 128
+WIDE = EXT + WO + WB
+CUTS = [(0, EXT + WO // 2), (EXT + WO // 2, WO // 2), (EXT + WO, WB // 2), (EXT + WO + WB // 2, WB // 2)]
+NCH = len(CUTS)
+BACK_ORDER = (2, 3, 0, 1)
+
+
+def features(f):
+    start, width = CUTS[f]
+    return (EXT, start + width) if f == 0 else (start, start + width)
+
+
 EXP_STEPS = [(dy, dc) for dy in (1, 3, 2, 0) for dc in (0, 1) if (dy, dc) != (0, 0)]
 
 
@@ -22,14 +32,18 @@
     return lax.dot_general(a, b, (dims, ((), ())), preferred_element_type=F32)
 
 
-def kernel(pay, pre, gate_hbm, up_hbm, down_hbm, tok_out, prob_out, down_out,
+def kernel(grad_in, weights_in, ids_in, places_in, pre_in, gate_hbm, up_hbm, down_hbm, tok_out, prob_out, down_out,
+           grad, weights, ids, places, pre, tok, prob, gdown,
            abuf, bbuf, frows, g, st, s, ysend, yrecv, psend, precv, xsend, xrecv, acc,
-           bsend, brecv, cbuf, arecv, arecv2, wgu, wdn,
-           load_sem, a_s, a_r, b_s, b_r, x_s, x_r, y_s, y_r, p_s, p_r, u_s, u_r, v_s, v_r, w_s, w_r):
+           bsend, brecv, cbuf, arecv, arecv2, wgu, wdn, zsend, zrecv,
+           load_sem, a_s, a_r, b_s, b_r, x_s, x_r, y_s, y_r, p_s, p_r, u_s, u_r, v_s, v_r, w_s, w_r, f_s, f_r, z_s, z_r):
     ex, et = lax.axis_index("exp"), lax.axis_index("et")
     y, core = ex // 2, ex % 2
     x, z = et // NZ, et % NZ
     q = z // 4
+    odd = z % 2
+    own_at = pl.multiple_of(WB + odd * WO, WO)
+    other_at = pl.multiple_of(WB + (1 - odd) * WO, WO)
     column = x * 2 + z // 16
     expert = ex * 8 + column
 
@@ -54,21 +68,33 @@
 
     sent = []
 
-    loads = [
-        pltpu.make_async_copy(gate_hbm.at[0], wgu.at[pl.ds(0, UNITS)], load_sem.at[0]),
-        pltpu.make_async_copy(up_hbm.at[0], wgu.at[pl.ds(128, UNITS)], load_sem.at[1]),
-        pltpu.make_async_copy(down_hbm.at[0], wdn.at[pl.ds(0, UNITS)], load_sem.at[2]),
-    ]
-    for load in loads:
-        load.start()
-
     barrier = pltpu.get_barrier_semaphore()
-    partners = [at_z(d) for d in (1, -1, 2, -2, 4, -4, 8, -8)]
+    partners = [at_z(d) for d in (8, -8, 4, -4, 2, -2, 1, -1)]
     partners += [at_x(d) for d in (1, 2, 3)]
     partners += [(exp_of(step), et) for step in EXP_STEPS]
     for device in partners:
         pl.semaphore_signal(barrier, inc=1, device_id=device, device_id_type=MESH)
-    abuf[:, pl.ds(q, 1)] = pay[...].reshape(3, 1, 16, 128)
+
+    early = [pltpu.make_async_copy(src, dst, load_sem.at[i]) for i, (src, dst) in enumerate(
+        ((grad_in, grad), (weights_in, weights), (ids_in, ids), (places_in, places)))]
+    loads = [pltpu.make_async_copy(pre_in, pre, load_sem.at[4])]
+    for i, (src, dst, row) in enumerate(((gate_hbm, wgu, 0), (up_hbm, wgu, 128), (down_hbm, wdn, 0))):
+        for j, (at, to, width) in enumerate(((own_at, 0, WO), (0, WO, WB), (other_at, WO + WB, WO))):
+            loads.append(pltpu.make_async_copy(
+                src.at[0, :, pl.ds(at, width)], dst.at[pl.ds(row, UNITS), pl.ds(to, width)],
+                load_sem.at[8 + i * 3 + j]))
+    for load in early + loads:
+        load.start()
+    for load in early:
+        load.wait()
+    for i in range(D // 128):
+        frows[i:i + 1, :] = grad[0:1, i * 128:(i + 1) * 128].astype(F32)
+    abuf[0:2, pl.ds(q, 1)] = frows[0:32].reshape(2, 1, 16, 128).astype(BF)
+    extra = jnp.concatenate(
+        [ids[...].astype(F32), places[...].astype(F32), weights[...].astype(F32),
+         jnp.zeros((1, EXT - 3 * TOPK), F32)], axis=1)
+    own_row = lax.broadcasted_iota(jnp.int32, (16, 128), 0) == q
+    abuf[2:3, pl.ds(q, 1)] = jnp.where(own_row, extra, 0.0).reshape(1, 1, 16, 128).astype(BF)
     pad = jnp.zeros((32, D), BF)
     wgu[pl.ds(UNITS, 32)] = pad
     wgu[pl.ds(128 + UNITS, 32)] = pad
@@ -107,12 +133,19 @@
             frows[(d * 2 + h) * 128:(d * 2 + h + 1) * 128] = (
                 bbuf[d, h * 9:h * 9 + 8].astype(F32).reshape(128, 128))
     gathers = []
+
+    def unit(u):
+        return jnp.concatenate(
+            [frows[pl.ds((d * 2 + u // 16) * 128 + u % 16, 8, stride=16), :] for d in range(4)], axis=0)
+
     for f, (start, width) in enumerate(CUTS):
-        h = f // 2
-        for i in range((f % 2) * 8, (f % 2) * 8 + 8):
-            row = jnp.concatenate(
-                [frows[pl.ds((d * 2 + h) * 128 + i, 8, stride=16), :] for d in range(4)], axis=0)
-            col = EXT + (h * 16 + i) * 128
+        begin, end = features(f)
+        for col in range(begin, end, 128):
+            v = (col - EXT) // 128
+            if v < OWN:
+                row = jnp.where(odd == 0, unit(BOTH + v), unit(BOTH + OWN + v))
+            else:
+                row = unit(v - OWN)
             g[0:32, col:col + 128] = row.astype(BF)
         cols = pl.ds(start, width)
         gathers.append([
@@ -152,7 +185,7 @@
     slot_col = lax.broadcasted_iota(jnp.int32, (ROWS, SLOTS), 1)
     place = (slot_row // PAD) * CAP + slot_row % PAD
     spread = jnp.where((place == slot_col) & (slot_row % PAD < CAP), 1.0, 0.0).astype(BF)
-    pre_rows = dot(spread, pre[...]).astype(BF)
+    pre_rows = dot(spread, pre[0], ((1,), (1,))).astype(BF)
     unit_row = lax.broadcasted_iota(jnp.int32, (2 * UNITS, 128), 0)
     unit_col = lax.broadcasted_iota(jnp.int32, (2 * UNITS, 128), 1)
     pick_gate = jnp.where((unit_row == unit_col) & (unit_col < UNITS), 1.0, 0.0).astype(BF)
@@ -165,13 +198,25 @@
     hidden = product.astype(BF).astype(F32)
     gate_factor = up_pre * sig * (1.0 + gate_pre * (1.0 - sig))
 
+    pair = at_z(1 - 2 * odd)
+    half = WO // 2
+    forwards = []
     back = jnp.zeros((ROWS, 128), F32)
-    for f, (start, width) in enumerate(CUTS):
+    for f in range(NCH):
+        begin, end = features(f)
         for copy in dispatch[f]:
             copy.wait_recv()
-        back = back + dot(yrecv[:, EXT + f * CHUNK:EXT + (f + 1) * CHUNK],
-                          wdn[:, f * CHUNK:(f + 1) * CHUNK], ((1,), (1,)))
+        if f < 2:
+            forwards.append(send(
+                yrecv.at[:, pl.ds(begin, half)], yrecv.at[:, pl.ds(WIDE + f * half, half)],
+                f_s.at[f], f_r.at[f], pair))
+        back = back + dot(yrecv[:, begin:end], wdn[:, begin - EXT:end - EXT], ((1,), (1,)))
         sent += dispatch[f] + gathers[f]
+    for f in range(2):
+        forwards[f].wait_recv()
+        begin = WIDE + f * half
+        back = back + dot(yrecv[:, begin:begin + half], wdn[:, begin - EXT:begin - EXT + half], ((1,), (1,)))
+    sent += forwards
 
     ext = yrecv[:, 0:EXT].astype(F32)
     lane = lax.broadcasted_iota(jnp.int32, (ROWS, EXT), 1)
@@ -183,11 +228,22 @@
     psend[:, 0:EXT] = jnp.where(named, part_prob, 0.0).astype(BF)
     weighted = jnp.transpose(weight * product).astype(BF)
 
-    combine = []
-    for f, (start, width) in enumerate(CUTS):
+    swaps = []
+    for f in range(2):
+        begin = WO + WB + f * half
+        zsend[:, f * half:(f + 1) * half] = dot(grads, wgu[:, begin:begin + half]).astype(BF)
+        part = pl.ds(f * half, half)
+        swaps.append(send(zsend.at[:, part], zrecv.at[:, part], z_s.at[f], z_r.at[f], pair))
+    combine = [None] * NCH
+    for f in BACK_ORDER:
+        start, width = CUTS[f]
+        begin, end = features(f)
         cols = pl.ds(start, width)
-        psend[:, EXT + f * CHUNK:EXT + (f + 1) * CHUNK] = dot(
-            grads, wgu[:, f * CHUNK:(f + 1) * CHUNK]).astype(BF)
+        part = dot(grads, wgu[:, begin - EXT:end - EXT])
+        if f < 2:
+            swaps[f].wait_recv()
+            part = part + zrecv[:, f * half:(f + 1) * half].astype(F32)
+        psend[:, begin:end] = part.astype(BF)
         copies = []
         for j, step in enumerate(EXP_STEPS):
             to = exp_of(step)
@@ -195,14 +251,17 @@
             copies.append(send(psend.at[rows, cols], precv.at[mine_rows, cols],
                                p_s.at[j, f], p_r.at[j, f], (to, et)))
         precv[mine_rows, start:start + width] = psend[mine_rows, start:start + width]
-        combine.append(copies)
-
-    for f in range(NCH):
-        down_out[:, f * CHUNK:(f + 1) * CHUNK] = dot(
-            weighted, yrecv[:, EXT + f * CHUNK:EXT + (f + 1) * CHUNK])[0:UNITS].astype(BF)
-
-    reduces = []
-    for f, (start, width) in enumerate(CUTS):
+        combine[f] = copies
+        if f == 3:
+            for at, begin, width in ((0, EXT + WO, WB), (own_at, EXT, WO), (other_at, WIDE, WO)):
+                gdown[:, pl.ds(at, width)] = dot(weighted, yrecv[:, begin:begin + width])[0:UNITS].astype(BF)
+    sent += swaps
+    stores = [pltpu.make_async_copy(gdown, down_out, load_sem.at[5])]
+    stores[0].start()
+
+    reduces = [None] * NCH
+    for f in BACK_ORDER:
+        start, width = CUTS[f]
         cols = pl.ds(start, width)
         for copy in combine[f]:
             copy.wait_recv()
@@ -210,11 +269,18 @@
         dense = dot(st[...], precv[:, start:start + width])
         acc[:, start:start + width] = dense[0:32]
         xsend[:, start:start + width] = dense[32:128].astype(BF)
-        reduces.append([
+        reduces[f] = [
             send(xsend.at[pl.ds((dx - 1) * 32, 32), cols], xrecv.at[dx - 1, :, cols],
                  u_s.at[dx - 1, f], u_r.at[dx - 1, f], at_x(dx))
-            for dx in (1, 2, 3)])
-    for f, (start, width) in enumerate(CUTS):
+            for dx in (1, 2, 3)]
+
+    def put(u, rows):
+        for d in range(4):
+            frows[pl.ds((d * 2 + u // 16) * 128 + u % 16, 8, stride=16), :] = rows[d * 8:d * 8 + 8]
+
+    for f in BACK_ORDER:
+        start, width = CUTS[f]
+        begin, end = features(f)
         for copy in reduces[f]:
             copy.wait_recv()
         sent += reduces[f]
@@ -223,12 +289,14 @@
             total = total + xrecv[i, :, start:start + width].astype(F32)
         if f == 0:
             ext_total = total[:, 0:EXT]
-            total = total[:, EXT:]
-        h = f // 2
-        for i in range(8):
-            for d in range(4):
-                frows[pl.ds((d * 2 + h) * 128 + (f % 2) * 8 + i, 8, stride=16), :] = (
-                    total[d * 8:d * 8 + 8, i * 128:(i + 1) * 128])
+        for col in range(begin, end, 128):
+            v = (col - EXT) // 128
+            rows = total[:, col - start:col - start + 128]
+            if v < OWN:
+                put(BOTH + v, jnp.where(odd == 0, rows, 0.0))
+                put(BOTH + OWN + v, jnp.where(odd == 0, 0.0, rows))
+            else:
+                put(v - OWN, rows)
 
     for d in range(1, 4):
         for h in range(2):
@@ -277,45 +345,70 @@
     for i in range(4):
         total = total + arecv[3 + i].astype(F32)
     total = total.reshape(3, 16, 128)
-    tok_out[...] = total[0:2].astype(BF)
-    prob_out[...] = total[2]
+    frows[0:32] = total[0:2].reshape(32, 128)
+    for i in range(D // 128):
+        tok[0:1, i * 128:(i + 1) * 128] = frows[i:i + 1, :].astype(BF)
+    prob[...] = jnp.sum(jnp.where(own_row, total[2], 0.0), axis=0, keepdims=True)[:, 0:TOPK]
+    for i, (src, dst) in enumerate(((tok, tok_out), (prob, prob_out))):
+        stores.append(pltpu.make_async_copy(src, dst, load_sem.at[6 + i]))
+        stores[-1].start()
     for copy in sent:
         copy.wait_send()
+    for store in stores:
+        store.wait()
+
+
+def deliver(tok, prob, down, tok_out, prob_out, down_out, tok_buf, prob_buf, down_buf, in_sem, out_sem):
+    parts = [(tok, tok_buf, tok_out), (prob, prob_buf, prob_out)]
+    for i in range(0, UNITS, 32):
+        rows = pl.ds(i, 32)
+        parts.append((down.at[rows], down_buf.at[rows], down_out.at[rows]))
+    ins = [pltpu.make_async_copy(src, buf, in_sem.at[i]) for i, (src, buf, _) in enumerate(parts)]
+    outs = [pltpu.make_async_copy(buf, dst, out_sem.at[i]) for i, (_, buf, dst) in enumerate(parts)]
+    for copy in ins:
+        copy.start()
+    for copy, onward in zip(ins, outs):
+        copy.wait()
+        onward.start()
+    for copy in outs:
+        copy.wait()
 
 
 def body(grad_out, route_weight, expert_ids, slot_ids, saved_pre, gate_proj, up_proj, down_proj):
-    q = lax.axis_index("et") % NZ // 4
-    extra = jnp.concatenate(
-        [expert_ids.astype(BF), slot_ids.astype(BF), route_weight, jnp.zeros((1, EXT - 3 * TOPK), BF)], axis=1)
-    extra = jnp.where(jnp.arange(16)[:, None] == q, extra, jnp.zeros((), BF))
-    pay = jnp.concatenate([grad_out.reshape(2, 16, 128), extra[None]], axis=0)
-    vmem = pl.BlockSpec(memory_space=pltpu.VMEM)
     hbm = pl.BlockSpec(memory_space=pl.ANY)
-    wide = EXT + D
     dma = lambda *shape: pltpu.SemaphoreType.DMA(shape)
-    tokens, probs, down_grad = pl.pallas_call(
+    outs = (
+        jax.ShapeDtypeStruct((1, D), BF),
+        jax.ShapeDtypeStruct((1, TOPK), F32),
+        jax.ShapeDtypeStruct((UNITS, D), BF),
+    )
+    results = pl.pallas_call(
         kernel,
-        out_shape=(
-            jax.ShapeDtypeStruct((2, 16, 128), BF),
-            jax.ShapeDtypeStruct((16, 128), F32),
-            jax.ShapeDtypeStruct((UNITS, D), BF),
-        ),
-        in_specs=[vmem, vmem, hbm, hbm, hbm],
-        out_specs=(vmem, vmem, vmem),
+        out_shape=outs,
+        in_specs=[hbm] * 8,
+        out_specs=(hbm,) * 3,
         scratch_shapes=[
+            pltpu.VMEM((1, D), BF),
+            pltpu.VMEM((1, TOPK), BF),
+            pltpu.VMEM((1, TOPK), jnp.int32),
+            pltpu.VMEM((1, TOPK), jnp.int32),
+            pltpu.VMEM((1, 2 * UNITS, SLOTS), BF),
+            pltpu.VMEM((1, D), BF),
+            pltpu.VMEM((1, TOPK), F32),
+            pltpu.VMEM((UNITS, D), BF),
             pltpu.VMEM((3, 8, 16, 128), BF),
             pltpu.VMEM((4, 17, 16, 128), BF),
             pltpu.VMEM((1024, 128), F32),
-            pltpu.VMEM((128, wide), BF),
+            pltpu.VMEM((128, WIDE), BF),
             pltpu.VMEM((128, ROWS), BF),
             pltpu.VMEM((ROWS, 128), BF),
-            pltpu.VMEM((ROWS, wide), BF),
-            pltpu.VMEM((ROWS, wide), BF),
-            pltpu.VMEM((ROWS, wide), BF),
-            pltpu.VMEM((ROWS, wide), BF),
-            pltpu.VMEM((96, wide), BF),
-            pltpu.VMEM((3, 32, wide), BF),
-            pltpu.VMEM((32, wide), F32),
+            pltpu.VMEM((ROWS, WIDE), BF),
+            pltpu.VMEM((ROWS, EXT + D), BF),
+            pltpu.VMEM((ROWS, WIDE), BF),
+            pltpu.VMEM((ROWS, WIDE), BF),
+            pltpu.VMEM((96, WIDE), BF),
+            pltpu.VMEM((3, 32, WIDE), BF),
+            pltpu.VMEM((32, WIDE), F32),
             pltpu.VMEM((3, 17, 16, 128), BF),
             pltpu.VMEM((3, 17, 16, 128), BF),
             pltpu.VMEM((3, 8, 16, 128), F32),
@@ -323,13 +416,24 @@
             pltpu.VMEM((3, 8, 16, 128), BF),
             pltpu.VMEM((256, D), BF),
             pltpu.VMEM((128, D), BF),
-            dma(3), dma(7), dma(7), dma(4), dma(4), dma(3, NCH), dma(3, NCH), dma(7, NCH), dma(7, NCH),
+            pltpu.VMEM((ROWS, WO), BF),
+            pltpu.VMEM((ROWS, WO), BF),
+            dma(17), dma(7), dma(7), dma(4), dma(4), dma(3, NCH), dma(3, NCH), dma(7, NCH), dma(7, NCH),
             dma(7, NCH), dma(7, NCH), dma(3, NCH), dma(3, NCH), dma(4), dma(4), dma(7), dma(7),
+            dma(2), dma(2), dma(2), dma(2),
         ],
         compiler_params=pltpu.CompilerParams(
-            collective_id=0, has_side_effects=True, vmem_limit_bytes=50 * 2**20),
-    )(pay, saved_pre[0], gate_proj, up_proj, down_proj)
-    return tokens.reshape(1, D), lax.dynamic_slice(probs, (q, 0), (1, TOPK)), down_grad[None]
+            collective_id=0, has_side_effects=True, vmem_limit_bytes=60 * 2**20),
+    )(grad_out, route_weight, expert_ids, slot_ids, jnp.swapaxes(saved_pre, 1, 2), gate_proj, up_proj, down_proj)
+    tokens, probs, down_grad = pl.pallas_call(
+        deliver,
+        out_shape=outs,
+        in_specs=[hbm] * 3,
+        out_specs=(hbm,) * 3,
+        scratch_shapes=[
+            pltpu.VMEM((1, D), BF), pltpu.VMEM((1, TOPK), F32), pltpu.VMEM((UNITS, D), BF), dma(5), dma(5)],
+    )(*results)
+    return tokens, probs, down_grad[None]
 
 
 def solution(mesh):

time: 136 us -> 121 us (0.89)
  Pallas kernels: 126 us -> 120 us
  local copies, waits for them, and re-layouts: 5.52 us -> 0 us
  other arithmetic: 2.91 us -> 0 us
    pallas_call x1 -> x2, Pallas kernels: 126 us -> 120 us  [the longest x1 118 us: body(): pl.pallas_call(kernel, out_shape=outs, in_specs=[hbm] * 8, out_specs=(hbm...]
    unnamed x10 -> x0, local copies, waits for them, and re-layouts: 4.38 us -> none
where the time goes in v2:
time: 121 us
  Pallas kernels  120 us (99%)
    pallas_call x1, Pallas kernels, body(): pl.pallas_call(kernel, out_shape=outs, in_specs=[hbm] * 8, out_specs=(hbm...  118 us

profile of v2, /device:TPU:6, one launch (start us, length us, event | category | flops | bytes accessed | tf_op | source)
XLA Modules:
  0.0 120.5 jit_solution(4770422070774790479)
XLA Ops:
  0.6 118.0 %shard_map.103 = (bf16[1,4096]{1,0:T(2,128)(2,1)}, f32[1,8]{1,0:T(1,128)}, bf16[96,4096]{1,0:T(8,128)(2,1)}) custom-call(bf16[1,4096]{1,0:T(2,128)(2,1)} %grad_in.1, bf16[1,8]{1,0:T(2,128)(2,1)} %weights_in.1, s32[1,8]{1,0:T(1,128)} %ids_in.1, s32[1,8]{1,0:T(1,128)} %places_in.1, bf16[1,192,240]{2,1,0:T(8,128)(2,1)} %bitcast.2, ...), custom_call_target="tpu_custom_call" | custom-call | tf_op jit(solution)/shard_map/pallas_call | solution.py:385
  118.6 1.9 %shard_map.104 = (bf16[1,4096]{1,0:T(2,128)(2,1)}, f32[1,8]{1,0:T(1,128)}, bf16[96,4096]{1,0:T(8,128)(2,1)}) custom-call(bf16[1,4096]{1,0:T(2,128)(2,1)} %get-tuple-element.9.tok, f32[1,8]{1,0:T(1,128)} %get-tuple-element.10.prob, bf16[96,4096]{1,0:T(8,128)(2,1)} %get-tuple-element.11.down), custom_call_target="tpu_custom_call" | custom-call | tf_op jit(solution)/shard_map/pallas_call | solution.py:428

commit v3 on v2

--- a/solution.py
+++ b/solution.py
@@ -11,7 +11,7 @@
 SLOTS, PAD, BLOCKS = 240, 32, 8
 ROWS = BLOCKS * PAD
 EXT = 128
-NX, NZ, NQ = 4, 32, 8
+NX, NZ = 4, 32
 OWN, BOTH = 8, 16
 WO, WB = OWN * 128, BOTH * 128
 WIDE = EXT + WO + WB
@@ -34,13 +34,13 @@
 
 def kernel(grad_in, weights_in, ids_in, places_in, pre_in, gate_hbm, up_hbm, down_hbm, tok_out, prob_out, down_out,
            grad, weights, ids, places, pre, tok, prob, gdown,
-           abuf, bbuf, frows, g, st, s, ysend, yrecv, psend, precv, xsend, xrecv, acc,
-           bsend, brecv, cbuf, arecv, arecv2, wgu, wdn, zsend, zrecv,
-           load_sem, a_s, a_r, b_s, b_r, x_s, x_r, y_s, y_r, p_s, p_r, u_s, u_r, v_s, v_r, w_s, w_r, f_s, f_r, z_s, z_r):
+           tokens, extras, ext_rows, frows, g, st, s, ysend, yrecv, psend, precv, xsend, xrecv, acc,
+           sums, sum_ext, near_in, near_ext, single_in, single_ext, total, total_ext, far_send, far_in, far_ext,
+           wgu, wdn, zsend, zrecv,
+           load_sem, n_s, n_r, x_s, x_r, y_s, y_r, p_s, p_r, u_s, u_r, f_s, f_r, z_s, z_r):
     ex, et = lax.axis_index("exp"), lax.axis_index("et")
     y, core = ex // 2, ex % 2
     x, z = et // NZ, et % NZ
-    q = z // 4
     odd = z % 2
     own_at = pl.multiple_of(WB + odd * WO, WO)
     other_at = pl.multiple_of(WB + (1 - odd) * WO, WO)
@@ -57,9 +57,6 @@
         dy, dc = step
         return lax.rem(y + dy, 4) * 2 + lax.rem(core + dc, 2)
 
-    def slot(j):
-        return lax.rem(q + j + NQ, NQ)
-
     def send(src, dst, ss, rs, device):
         copy = pltpu.make_async_remote_copy(
             src_ref=src, dst_ref=dst, send_sem=ss, recv_sem=rs, device_id=device, device_id_type=MESH)
@@ -67,9 +64,20 @@
         return copy
 
     sent = []
+    used = [0]
+
+    def z_copy(src, dst, dz):
+        i = used[0]
+        used[0] += 1
+        return send(src, dst, n_s.at[i], n_r.at[i], at_z(dz))
+
+    def arrived(copies):
+        for copy in copies:
+            copy.wait_recv()
+        sent.extend(copies)
 
     barrier = pltpu.get_barrier_semaphore()
-    partners = [at_z(d) for d in (8, -8, 4, -4, 2, -2, 1, -1)]
+    partners = [at_z(d) for d in (4, -4, 3, -3, 2, -2, 1, -1)]
     partners += [at_x(d) for d in (1, 2, 3)]
     partners += [(exp_of(step), et) for step in EXP_STEPS]
     for device in partners:
@@ -89,49 +97,39 @@
         load.wait()
     for i in range(D // 128):
         frows[i:i + 1, :] = grad[0:1, i * 128:(i + 1) * 128].astype(F32)
-    abuf[0:2, pl.ds(q, 1)] = frows[0:32].reshape(2, 1, 16, 128).astype(BF)
-    extra = jnp.concatenate(
+    tokens[0, :, 3] = frows[0:32].reshape(2, 16, 128).astype(BF)
+    extras[0, 3] = jnp.concatenate(
         [ids[...].astype(F32), places[...].astype(F32), weights[...].astype(F32),
          jnp.zeros((1, EXT - 3 * TOPK), F32)], axis=1)
-    own_row = lax.broadcasted_iota(jnp.int32, (16, 128), 0) == q
-    abuf[2:3, pl.ds(q, 1)] = jnp.where(own_row, extra, 0.0).reshape(1, 1, 16, 128).astype(BF)
+    near_in[2, 1, 0] = jnp.zeros((16, 128), BF)
     pad = jnp.zeros((32, D), BF)
     wgu[pl.ds(UNITS, 32)] = pad
     wgu[pl.ds(128 + UNITS, 32)] = pad
     wdn[pl.ds(UNITS, 32)] = pad
     pl.semaphore_wait(barrier, len(partners))
 
-    mine = abuf.at[:, pl.ds(q, 1)]
-    first = [send(mine, mine, a_s.at[i], a_r.at[i], at_z(d)) for i, d in enumerate((4, -4, 8, -8))]
-    for copy in first:
-        copy.wait_recv()
-    second = []
-    for i, (j, d) in enumerate(((1, -8), (2, -8), (-1, 8))):
-        part = abuf.at[:, pl.ds(slot(j), 1)]
-        second.append(send(part, part, a_s.at[4 + i], a_r.at[4 + i], at_z(d)))
-    for copy in second:
-        copy.wait_recv()
-    sent += first + second
-
-    bbuf[0, 0:8] = abuf[0]
-    bbuf[0, 8] = jnp.sum(abuf[2].astype(F32), axis=0).astype(BF)
-    bbuf[0, 9:17] = abuf[1]
-    low, high = pl.ds(0, 9), pl.ds(9, 8)
-    near = [
-        send(bbuf.at[0], bbuf.at[1], b_s.at[0], b_r.at[0], at_z(-1)),
-        send(bbuf.at[0], bbuf.at[3], b_s.at[1], b_r.at[1], at_z(1)),
-        send(bbuf.at[0, low], bbuf.at[2, low], b_s.at[2], b_r.at[2], at_z(-2)),
-        send(bbuf.at[0, high], bbuf.at[2, high], b_s.at[3], b_r.at[3], at_z(2)),
-    ]
-    for copy in near:
-        copy.wait_recv()
-    sent += near
+    def both(cls, at, to_cls, to, count, dz):
+        return [
+            z_copy(tokens.at[cls, :, pl.ds(at, count)], tokens.at[to_cls, :, pl.ds(to, count)], dz),
+            z_copy(extras.at[cls, pl.ds(at, count)], extras.at[to_cls, pl.ds(to, count)], dz)]
+
+    arrived(both(0, 3, 0, 2, 1, 4) + both(0, 3, 0, 4, 1, -4))
+    arrived(both(0, 3, 0, 5, 2, -8) + both(0, 2, 0, 0, 2, 8))
+
+    arrived(
+        both(0, 0, 1, 0, 7, -1) + both(0, 0, 3, 0, 7, 1)
+        + [z_copy(tokens.at[0, 0, pl.ds(0, 7)], tokens.at[2, 0, pl.ds(0, 7)], -2),
+           z_copy(tokens.at[0, 1, pl.ds(1, 6)], tokens.at[2, 1, pl.ds(0, 6)], 2),
+           z_copy(tokens.at[0, 1, pl.ds(6, 1)], tokens.at[2, 1, pl.ds(6, 1)], -2),
+           z_copy(extras.at[0, pl.ds(0, 7)], extras.at[2, pl.ds(0, 7)], -2)]
+        + both(0, 0, 2, 7, 1, 2) + both(0, 0, 1, 7, 1, 3) + both(0, 6, 3, 7, 1, -3) + both(0, 6, 0, 7, 1, -4))
 
     for d in range(4):
-        g[d * 8:d * 8 + 8, 0:EXT] = bbuf[d, 8, 0:8]
+        for i in range(8):
+            ext_rows[d * 8 + i:d * 8 + i + 1, :] = extras[d, i]
         for h in range(2):
-            frows[(d * 2 + h) * 128:(d * 2 + h + 1) * 128] = (
-                bbuf[d, h * 9:h * 9 + 8].astype(F32).reshape(128, 128))
+            frows[(d * 2 + h) * 128:(d * 2 + h + 1) * 128] = tokens[d, h].astype(F32).reshape(128, 128)
+    g[0:32, 0:EXT] = ext_rows[...].astype(BF)
     gathers = []
 
     def unit(u):
@@ -284,71 +282,83 @@
         for copy in reduces[f]:
             copy.wait_recv()
         sent += reduces[f]
-        total = acc[:, start:start + width]
+        whole = acc[:, start:start + width]
         for i in range(3):
-            total = total + xrecv[i, :, start:start + width].astype(F32)
+            whole = whole + xrecv[i, :, start:start + width].astype(F32)
         if f == 0:
-            ext_total = total[:, 0:EXT]
+            ext_total = whole[:, 0:EXT]
         for col in range(begin, end, 128):
             v = (col - EXT) // 128
-            rows = total[:, col - start:col - start + 128]
+            rows = whole[:, col - start:col - start + 128]
             if v < OWN:
                 put(BOTH + v, jnp.where(odd == 0, rows, 0.0))
                 put(BOTH + OWN + v, jnp.where(odd == 0, 0.0, rows))
             else:
                 put(v - OWN, rows)
 
-    for d in range(1, 4):
+    for d in range(4):
         for h in range(2):
-            bsend[d - 1, h * 9:h * 9 + 8] = (
-                frows[(d * 2 + h) * 128:(d * 2 + h + 1) * 128].reshape(8, 16, 128).astype(BF))
-        bsend[d - 1, 8] = jnp.concatenate(
-            [ext_total[d * 8:d * 8 + 8], jnp.zeros((8, 128), F32)], axis=0).astype(BF)
-    near = [
-        send(bsend.at[0], brecv.at[0], v_s.at[0], v_r.at[0], at_z(1)),
-        send(bsend.at[2], brecv.at[1], v_s.at[1], v_r.at[1], at_z(-1)),
-        send(bsend.at[1, low], brecv.at[2, low], v_s.at[2], v_r.at[2], at_z(2)),
-        send(bsend.at[1, high], brecv.at[2, high], v_s.at[3], v_r.at[3], at_z(-2)),
-    ]
-    for copy in near:
-        copy.wait_recv()
-    sent += near
+            if d:
+                sums[d, h] = frows[(d * 2 + h) * 128:(d * 2 + h + 1) * 128].reshape(8, 16, 128).astype(BF)
+            else:
+                sums[d, h, 7] = frows[h * 128 + 112:h * 128 + 128].astype(BF)
+        for i in range(8):
+            sum_ext[d, i] = ext_total[d * 8 + i:d * 8 + i + 1]
+
+    def seven(cls, to, dz):
+        return [z_copy(sums.at[cls, :, pl.ds(0, 7)], near_in.at[to, :, pl.ds(0, 7)], dz),
+                z_copy(sum_ext.at[cls, pl.ds(0, 7)], near_ext.at[to], dz)]
+
+    def eighth(cls, to, dz):
+        return [z_copy(sums.at[cls, :, pl.ds(7, 1)], single_in.at[to], dz),
+                z_copy(sum_ext.at[cls, pl.ds(7, 1)], single_ext.at[to], dz)]
+
+    arrived(
+        seven(1, 0, 1) + seven(3, 1, -1)
+        + [z_copy(sums.at[2, 0, pl.ds(0, 7)], near_in.at[2, 0, pl.ds(0, 7)], 2),
+           z_copy(sums.at[2, 1, pl.ds(0, 6)], near_in.at[2, 1, pl.ds(1, 6)], -2),
+           z_copy(sums.at[2, 1, pl.ds(6, 1)], single_in.at[4, 1], 2),
+           z_copy(sum_ext.at[2, pl.ds(0, 7)], near_ext.at[2], 2)]
+        + eighth(2, 0, -2) + eighth(1, 1, -3) + eighth(3, 2, 3) + eighth(0, 3, 4))
     for h in range(2):
-        total = frows[h * 128:(h + 1) * 128].reshape(8, 16, 128)
+        rows = frows[h * 128:h * 128 + 112].reshape(7, 16, 128)
         for i in range(3):
-            total = total + brecv[i, h * 9:h * 9 + 8].astype(F32)
-        cbuf[h] = total
-    total = jnp.concatenate([ext_total[0:8], jnp.zeros((8, 128), F32)], axis=0)
+            rows = rows + near_in[i, h, 0:7].astype(F32)
+        total[h] = rows
+    rows = sum_ext[0, 0:7]
     for i in range(3):
-        total = total + brecv[i, 8].astype(F32)
-    for j in range(8):
-        cbuf[2, j] = total
-
-    for j in range(8):
-        arecv2[:, j] = cbuf[:, j].astype(BF)
-    third = []
-    for i, (j, d) in enumerate(((3, 8), (4, 8), (-3, -8))):
-        third.append(send(arecv2.at[:, pl.ds(slot(j), 1)], arecv.at[i], w_s.at[i], w_r.at[i], at_z(d)))
-    for copy in third:
-        copy.wait_recv()
-    for i, j in enumerate((1, 2, -1)):
-        part = cbuf[:, pl.ds(slot(j), 1)] + arecv[i].astype(F32)
-        arecv2[:, pl.ds(slot(j), 1)] = part.astype(BF)
-    fourth = []
-    for i, (j, d) in enumerate(((1, 4), (-1, -4), (2, 8), (-2, -8))):
-        fourth.append(send(arecv2.at[:, pl.ds(slot(j), 1)], arecv.at[3 + i],
-                           w_s.at[3 + i], w_r.at[3 + i], at_z(d)))
-    for copy in fourth:
-        copy.wait_recv()
-    sent += third + fourth
-    total = cbuf[:, pl.ds(q, 1)]
-    for i in range(4):
-        total = total + arecv[3 + i].astype(F32)
-    total = total.reshape(3, 16, 128)
-    frows[0:32] = total[0:2].reshape(32, 128)
+        rows = rows + near_ext[i]
+    total_ext[...] = rows
+    for place, left in ((0, (0, 1)), (6, (2, 3))):
+        for i in left:
+            total[:, place] = total[:, place] + single_in[i, :, 0].astype(F32)
+            total_ext[place] = total_ext[place] + single_ext[i, 0]
+    total[1, 6] = total[1, 6] + single_in[4, 1, 0].astype(F32)
+
+    far_send[...] = total[...].astype(BF)
+
+    def back_far(at, to, count, dz):
+        return [z_copy(far_send.at[:, pl.ds(at, count)], far_in.at[to, :, pl.ds(0, count)], dz),
+                z_copy(total_ext.at[pl.ds(at, count)], far_ext.at[to, pl.ds(0, count)], dz)]
+
+    arrived(back_far(5, 0, 2, 8) + back_far(0, 1, 2, -8))
+    far_send[:, 2] = (total[:, 2] + far_in[1, :, 0].astype(F32)).astype(BF)
+    far_send[:, 4] = (total[:, 4] + far_in[0, :, 1].astype(F32)).astype(BF)
+    last = total[:, 3] + far_in[0, :, 0].astype(F32) + far_in[1, :, 1].astype(F32)
+    last_ext = total_ext[3] + far_ext[0, 0] + far_ext[1, 1]
+    far_ext[2, 1] = total_ext[2] + far_ext[1, 0]
+    far_ext[3, 1] = total_ext[4] + far_ext[0, 1]
+    arrived([
+        z_copy(far_send.at[:, pl.ds(2, 1)], far_in.at[2, :, pl.ds(0, 1)], -4),
+        z_copy(far_ext.at[2, pl.ds(1, 1)], far_ext.at[2, pl.ds(0, 1)], -4),
+        z_copy(far_send.at[:, pl.ds(4, 1)], far_in.at[3, :, pl.ds(0, 1)], 4),
+        z_copy(far_ext.at[3, pl.ds(1, 1)], far_ext.at[3, pl.ds(0, 1)], 4)])
+    last = last + far_in[2, :, 0].astype(F32) + far_in[3, :, 0].astype(F32)
+    last_ext = last_ext + far_ext[2, 0] + far_ext[3, 0]
+    frows[0:32] = last.reshape(32, 128)
     for i in range(D // 128):
         tok[0:1, i * 128:(i + 1) * 128] = frows[i:i + 1, :].astype(BF)
-    prob[...] = jnp.sum(jnp.where(own_row, total[2], 0.0), axis=0, keepdims=True)[:, 0:TOPK]
+    prob[...] = last_ext[:, 0:TOPK]
     for i, (src, dst) in enumerate(((tok, tok_out), (prob, prob_out))):
         stores.append(pltpu.make_async_copy(src, dst, load_sem.at[6 + i]))
         stores[-1].start()
@@ -396,8 +406,9 @@
             pltpu.VMEM((1, D), BF),
             pltpu.VMEM((1, TOPK), F32),
             pltpu.VMEM((UNITS, D), BF),
-            pltpu.VMEM((3, 8, 16, 128), BF),
-            pltpu.VMEM((4, 17, 16, 128), BF),
+            pltpu.VMEM((4, 2, 8, 16, 128), BF),
+            pltpu.VMEM((4, 8, 1, 128), F32),
+            pltpu.VMEM((32, 128), F32),
             pltpu.VMEM((1024, 128), F32),
             pltpu.VMEM((128, WIDE), BF),
             pltpu.VMEM((128, ROWS), BF),
@@ -409,17 +420,23 @@
             pltpu.VMEM((96, WIDE), BF),
             pltpu.VMEM((3, 32, WIDE), BF),
             pltpu.VMEM((32, WIDE), F32),
-            pltpu.VMEM((3, 17, 16, 128), BF),
-            pltpu.VMEM((3, 17, 16, 128), BF),
-            pltpu.VMEM((3, 8, 16, 128), F32),
-            pltpu.VMEM((7, 3, 1, 16, 128), BF),
-            pltpu.VMEM((3, 8, 16, 128), BF),
+            pltpu.VMEM((4, 2, 8, 16, 128), BF),
+            pltpu.VMEM((4, 8, 1, 128), F32),
+            pltpu.VMEM((3, 2, 7, 16, 128), BF),
+            pltpu.VMEM((3, 7, 1, 128), F32),
+            pltpu.VMEM((5, 2, 1, 16, 128), BF),
+            pltpu.VMEM((4, 1, 1, 128), F32),
+            pltpu.VMEM((2, 7, 16, 128), F32),
+            pltpu.VMEM((7, 1, 128), F32),
+            pltpu.VMEM((2, 7, 16, 128), BF),
+            pltpu.VMEM((4, 2, 2, 16, 128), BF),
+            pltpu.VMEM((4, 2, 1, 128), F32),
             pltpu.VMEM((256, D), BF),
             pltpu.VMEM((128, D), BF),
             pltpu.VMEM((ROWS, WO), BF),
             pltpu.VMEM((ROWS, WO), BF),
-            dma(17), dma(7), dma(7), dma(4), dma(4), dma(3, NCH), dma(3, NCH), dma(7, NCH), dma(7, NCH),
-            dma(7, NCH), dma(7, NCH), dma(3, NCH), dma(3, NCH), dma(4), dma(4), dma(7), dma(7),
+            dma(17), dma(64), dma(64), dma(3, NCH), dma(3, NCH), dma(7, NCH), dma(7, NCH),
+            dma(7, NCH), dma(7, NCH), dma(3, NCH), dma(3, NCH),
             dma(2), dma(2), dma(2), dma(2),
         ],
         compiler_params=pltpu.CompilerParams(

time: 121 us -> 116 us (0.959)
  Pallas kernels: 120 us -> 115 us
    pallas_call x1, Pallas kernels: 118 us -> 113 us  [body(): pl.pallas_call(kernel, out_shape=outs, in_specs=[hbm] * 8, out_specs=(hbm...]
where the time goes in v3:
time: 116 us; the launch traced here: 115 us
  Pallas kernels  115 us (99%)
    pallas_call x1, Pallas kernels, body(): pl.pallas_call(kernel, out_shape=outs, in_specs=[hbm] * 8, out_specs=(hbm...  113 us

profile of v3, /device:TPU:6, one launch (start us, length us, event | category | flops | bytes accessed | tf_op | source)
XLA Modules:
  0.0 115.2 jit_solution(8174079765949358475)
XLA Ops:
  0.6 112.7 %shard_map.103 = (bf16[1,4096]{1,0:T(2,128)(2,1)}, f32[1,8]{1,0:T(1,128)}, bf16[96,4096]{1,0:T(8,128)(2,1)}) custom-call(bf16[1,4096]{1,0:T(2,128)(2,1)} %grad_in.1, bf16[1,8]{1,0:T(2,128)(2,1)} %weights_in.1, s32[1,8]{1,0:T(1,128)} %ids_in.1, s32[1,8]{1,0:T(1,128)} %places_in.1, bf16[1,192,240]{2,1,0:T(8,128)(2,1)} %bitcast.2, ...), custom_call_target="tpu_custom_call" | custom-call | tf_op jit(solution)/shard_map/pallas_call | solution.py:395
  113.3 1.9 %shard_map.104 = (bf16[1,4096]{1,0:T(2,128)(2,1)}, f32[1,8]{1,0:T(1,128)}, bf16[96,4096]{1,0:T(8,128)(2,1)}) custom-call(bf16[1,4096]{1,0:T(2,128)(2,1)} %get-tuple-element.9.tok, f32[1,8]{1,0:T(1,128)} %get-tuple-element.10.prob, bf16[96,4096]{1,0:T(8,128)(2,1)} %get-tuple-element.11.down), custom_call_target="tpu_custom_call" | custom-call | tf_op jit(solution)/shard_map/pallas_call | solution.py:445

commit v4 on v3

--- a/solution.py
+++ b/solution.py
@@ -108,27 +108,40 @@
     wdn[pl.ds(UNITS, 32)] = pad
     pl.semaphore_wait(barrier, len(partners))
 
-    def both(cls, at, to_cls, to, count, dz):
-        return [
-            z_copy(tokens.at[cls, :, pl.ds(at, count)], tokens.at[to_cls, :, pl.ds(to, count)], dz),
-            z_copy(extras.at[cls, pl.ds(at, count)], extras.at[to_cls, pl.ds(to, count)], dz)]
-
-    arrived(both(0, 3, 0, 2, 1, 4) + both(0, 3, 0, 4, 1, -4))
-    arrived(both(0, 3, 0, 5, 2, -8) + both(0, 2, 0, 0, 2, 8))
-
-    arrived(
-        both(0, 0, 1, 0, 7, -1) + both(0, 0, 3, 0, 7, 1)
-        + [z_copy(tokens.at[0, 0, pl.ds(0, 7)], tokens.at[2, 0, pl.ds(0, 7)], -2),
-           z_copy(tokens.at[0, 1, pl.ds(1, 6)], tokens.at[2, 1, pl.ds(0, 6)], 2),
-           z_copy(tokens.at[0, 1, pl.ds(6, 1)], tokens.at[2, 1, pl.ds(6, 1)], -2),
-           z_copy(extras.at[0, pl.ds(0, 7)], extras.at[2, pl.ds(0, 7)], -2)]
-        + both(0, 0, 2, 7, 1, 2) + both(0, 0, 1, 7, 1, 3) + both(0, 6, 3, 7, 1, -3) + both(0, 6, 0, 7, 1, -4))
-
+    def feats(h, cls, at, to_cls, to, count, dz):
+        return z_copy(tokens.at[cls, h, pl.ds(at, count)], tokens.at[to_cls, h, pl.ds(to, count)], dz)
+
+    def sides(cls, at, to_cls, to, count, dz):
+        return z_copy(extras.at[cls, pl.ds(at, count)], extras.at[to_cls, pl.ds(to, count)], dz)
+
+    def move(h, moves):
+        return [feats(h, *m) for m in moves] + ([sides(*m) for m in moves] if h else [])
+
+    halves = (1, 0)
+    quarter = {h: move(h, [(0, 3, 0, 2, 1, 4), (0, 3, 0, 4, 1, -4)]) for h in halves}
+    eighths, near = {}, {}
+    for h in halves:
+        arrived(quarter[h])
+        eighths[h] = move(h, [(0, 3, 0, 5, 2, -8), (0, 2, 0, 0, 2, 8)])
+
+    for h in halves:
+        arrived(eighths[h])
+        near[h] = move(h, [(0, 6, 0, 7, 1, -4), (0, 0, 1, 7, 1, 3), (0, 6, 3, 7, 1, -3), (0, 0, 2, 7, 1, 2),
+                           (0, 0, 1, 0, 7, -1), (0, 0, 3, 0, 7, 1)])
+        if h:
+            near[h] += [feats(h, 0, 1, 2, 0, 6, 2), feats(h, 0, 6, 2, 6, 1, -2), sides(0, 0, 2, 0, 7, -2)]
+        else:
+            near[h] += [feats(h, 0, 0, 2, 0, 7, -2)]
+
+    def spread_rows(h):
+        arrived(near[h])
+        for d in range(4):
+            frows[(d * 2 + h) * 128:(d * 2 + h + 1) * 128] = tokens[d, h].astype(F32).reshape(128, 128)
+
+    spread_rows(1)
     for d in range(4):
         for i in range(8):
             ext_rows[d * 8 + i:d * 8 + i + 1, :] = extras[d, i]
-        for h in range(2):
-            frows[(d * 2 + h) * 128:(d * 2 + h + 1) * 128] = tokens[d, h].astype(F32).reshape(128, 128)
     g[0:32, 0:EXT] = ext_rows[...].astype(BF)
     gathers = []
 
@@ -138,6 +151,8 @@
 
     for f, (start, width) in enumerate(CUTS):
         begin, end = features(f)
+        if f == 2:
+            spread_rows(0)
         for col in range(begin, end, 128):
             v = (col - EXT) // 128
             if v < OWN:
@@ -258,12 +273,11 @@
     stores[0].start()
 
     reduces = [None] * NCH
-    for f in BACK_ORDER:
+
+    def combine_rows(f):
         start, width = CUTS[f]
         cols = pl.ds(start, width)
-        for copy in combine[f]:
-            copy.wait_recv()
-        sent += combine[f]
+        arrived(combine[f])
         dense = dot(st[...], precv[:, start:start + width])
         acc[:, start:start + width] = dense[0:32]
         xsend[:, start:start + width] = dense[32:128].astype(BF)
@@ -276,17 +290,17 @@
         for d in range(4):
             frows[pl.ds((d * 2 + u // 16) * 128 + u % 16, 8, stride=16), :] = rows[d * 8:d * 8 + 8]
 
-    for f in BACK_ORDER:
+    def sum_rows(f):
         start, width = CUTS[f]
         begin, end = features(f)
-        for copy in reduces[f]:
-            copy.wait_recv()
-        sent += reduces[f]
+        arrived(reduces[f])
         whole = acc[:, start:start + width]
         for i in range(3):
             whole = whole + xrecv[i, :, start:start + width].astype(F32)
         if f == 0:
-            ext_total = whole[:, 0:EXT]
+            for d in range(4):
+                for i in range(8):
+                    sum_ext[d, i] = whole[d * 8 + i:d * 8 + i + 1, 0:EXT]
         for col in range(begin, end, 128):
             v = (col - EXT) // 128
             rows = whole[:, col - start:col - start + 128]
@@ -296,69 +310,89 @@
             else:
                 put(v - OWN, rows)
 
-    for d in range(4):
-        for h in range(2):
+    def send_near(h):
+        for d in range(4):
             if d:
                 sums[d, h] = frows[(d * 2 + h) * 128:(d * 2 + h + 1) * 128].reshape(8, 16, 128).astype(BF)
             else:
                 sums[d, h, 7] = frows[h * 128 + 112:h * 128 + 128].astype(BF)
-        for i in range(8):
-            sum_ext[d, i] = ext_total[d * 8 + i:d * 8 + i + 1]
-
-    def seven(cls, to, dz):
-        return [z_copy(sums.at[cls, :, pl.ds(0, 7)], near_in.at[to, :, pl.ds(0, 7)], dz),
-                z_copy(sum_ext.at[cls, pl.ds(0, 7)], near_ext.at[to], dz)]
-
-    def eighth(cls, to, dz):
-        return [z_copy(sums.at[cls, :, pl.ds(7, 1)], single_in.at[to], dz),
-                z_copy(sum_ext.at[cls, pl.ds(7, 1)], single_ext.at[to], dz)]
-
-    arrived(
-        seven(1, 0, 1) + seven(3, 1, -1)
-        + [z_copy(sums.at[2, 0, pl.ds(0, 7)], near_in.at[2, 0, pl.ds(0, 7)], 2),
-           z_copy(sums.at[2, 1, pl.ds(0, 6)], near_in.at[2, 1, pl.ds(1, 6)], -2),
-           z_copy(sums.at[2, 1, pl.ds(6, 1)], single_in.at[4, 1], 2),
-           z_copy(sum_ext.at[2, pl.ds(0, 7)], near_ext.at[2], 2)]
-        + eighth(2, 0, -2) + eighth(1, 1, -3) + eighth(3, 2, 3) + eighth(0, 3, 4))
-    for h in range(2):
+        copies = []
+        for cls, to, dz in ((0, 3, 4), (1, 1, -3), (3, 2, 3), (2, 0, -2)):
+            copies.append(z_copy(sums.at[cls, h, pl.ds(7, 1)], single_in.at[to, h], dz))
+            if h:
+                copies.append(z_copy(sum_ext.at[cls, pl.ds(7, 1)], single_ext.at[to], dz))
+        for cls, to, dz in ((1, 0, 1), (3, 1, -1), (2, 2, 2)):
+            if cls != 2 or h == 0:
+                copies.append(z_copy(sums.at[cls, h, pl.ds(0, 7)], near_in.at[to, h, pl.ds(0, 7)], dz))
+            if h:
+                copies.append(z_copy(sum_ext.at[cls, pl.ds(0, 7)], near_ext.at[to], dz))
+        if h:
+            copies.append(z_copy(sums.at[2, 1, pl.ds(0, 6)], near_in.at[2, 1, pl.ds(1, 6)], -2))
+            copies.append(z_copy(sums.at[2, 1, pl.ds(6, 1)], single_in.at[4, 1], 2))
+        return copies
+
+    combine_rows(2)
+    combine_rows(3)
+    combine_rows(0)
+    sum_rows(2)
+    sum_rows(3)
+    near = {0: send_near(0)}
+    combine_rows(1)
+    sum_rows(0)
+    sum_rows(1)
+    near[1] = send_near(1)
+
+    def send_far(h):
+        arrived(near[h])
         rows = frows[h * 128:h * 128 + 112].reshape(7, 16, 128)
         for i in range(3):
             rows = rows + near_in[i, h, 0:7].astype(F32)
         total[h] = rows
-    rows = sum_ext[0, 0:7]
-    for i in range(3):
-        rows = rows + near_ext[i]
-    total_ext[...] = rows
-    for place, left in ((0, (0, 1)), (6, (2, 3))):
-        for i in left:
-            total[:, place] = total[:, place] + single_in[i, :, 0].astype(F32)
-            total_ext[place] = total_ext[place] + single_ext[i, 0]
-    total[1, 6] = total[1, 6] + single_in[4, 1, 0].astype(F32)
-
-    far_send[...] = total[...].astype(BF)
-
-    def back_far(at, to, count, dz):
-        return [z_copy(far_send.at[:, pl.ds(at, count)], far_in.at[to, :, pl.ds(0, count)], dz),
-                z_copy(total_ext.at[pl.ds(at, count)], far_ext.at[to, pl.ds(0, count)], dz)]
-
-    arrived(back_far(5, 0, 2, 8) + back_far(0, 1, 2, -8))
-    far_send[:, 2] = (total[:, 2] + far_in[1, :, 0].astype(F32)).astype(BF)
-    far_send[:, 4] = (total[:, 4] + far_in[0, :, 1].astype(F32)).astype(BF)
-    last = total[:, 3] + far_in[0, :, 0].astype(F32) + far_in[1, :, 1].astype(F32)
-    last_ext = total_ext[3] + far_ext[0, 0] + far_ext[1, 1]
-    far_ext[2, 1] = total_ext[2] + far_ext[1, 0]
-    far_ext[3, 1] = total_ext[4] + far_ext[0, 1]
-    arrived([
-        z_copy(far_send.at[:, pl.ds(2, 1)], far_in.at[2, :, pl.ds(0, 1)], -4),
-        z_copy(far_ext.at[2, pl.ds(1, 1)], far_ext.at[2, pl.ds(0, 1)], -4),
-        z_copy(far_send.at[:, pl.ds(4, 1)], far_in.at[3, :, pl.ds(0, 1)], 4),
-        z_copy(far_ext.at[3, pl.ds(1, 1)], far_ext.at[3, pl.ds(0, 1)], 4)])
-    last = last + far_in[2, :, 0].astype(F32) + far_in[3, :, 0].astype(F32)
-    last_ext = last_ext + far_ext[2, 0] + far_ext[3, 0]
-    frows[0:32] = last.reshape(32, 128)
+        for place, left in ((0, (0, 1)), (6, (2, 3))):
+            for i in left:
+                total[h, place] = total[h, place] + single_in[i, h, 0].astype(F32)
+        if h:
+            total[1, 6] = total[1, 6] + single_in[4, 1, 0].astype(F32)
+            rows = sum_ext[0, 0:7]
+            for i in range(3):
+                rows = rows + near_ext[i]
+            total_ext[...] = rows
+            for place, left in ((0, (0, 1)), (6, (2, 3))):
+                for i in left:
+                    total_ext[place] = total_ext[place] + single_ext[i, 0]
+        far_send[h] = total[h].astype(BF)
+        copies = []
+        for at, to, dz in ((5, 0, 8), (0, 1, -8)):
+            copies.append(z_copy(far_send.at[h, pl.ds(at, 2)], far_in.at[to, h], dz))
+            if h:
+                copies.append(z_copy(total_ext.at[pl.ds(at, 2)], far_ext.at[to], dz))
+        return copies
+
+    far = {h: send_far(h) for h in (0, 1)}
+
+    def send_last(h):
+        arrived(far[h])
+        far_send[h, 2] = (total[h, 2] + far_in[1, h, 0].astype(F32)).astype(BF)
+        far_send[h, 4] = (total[h, 4] + far_in[0, h, 1].astype(F32)).astype(BF)
+        total[h, 3] = total[h, 3] + far_in[0, h, 0].astype(F32) + far_in[1, h, 1].astype(F32)
+        if h:
+            total_ext[2] = total_ext[2] + far_ext[1, 0]
+            total_ext[4] = total_ext[4] + far_ext[0, 1]
+            total_ext[3] = total_ext[3] + far_ext[0, 0] + far_ext[1, 1]
+        copies = []
+        for at, to, dz in ((2, 2, -4), (4, 3, 4)):
+            copies.append(z_copy(far_send.at[h, pl.ds(at, 1)], far_in.at[to, h, pl.ds(0, 1)], dz))
+            if h:
+                copies.append(z_copy(total_ext.at[pl.ds(at, 1)], far_ext.at[to, pl.ds(0, 1)], dz))
+        return copies
+
+    last = {h: send_last(h) for h in (0, 1)}
+    for h in (0, 1):
+        arrived(last[h])
+        frows[h * 16:h * 16 + 16] = total[h, 3] + far_in[2, h, 0].astype(F32) + far_in[3, h, 0].astype(F32)
     for i in range(D // 128):
         tok[0:1, i * 128:(i + 1) * 128] = frows[i:i + 1, :].astype(BF)
-    prob[...] = last_ext[:, 0:TOPK]
+    prob[...] = (total_ext[3] + far_ext[2, 0] + far_ext[3, 0])[:, 0:TOPK]
     for i, (src, dst) in enumerate(((tok, tok_out), (prob, prob_out))):
         stores.append(pltpu.make_async_copy(src, dst, load_sem.at[6 + i]))
         stores[-1].start()
@@ -435,7 +469,7 @@
             pltpu.VMEM((128, D), BF),
             pltpu.VMEM((ROWS, WO), BF),
             pltpu.VMEM((ROWS, WO), BF),
-            dma(17), dma(64), dma(64), dma(3, NCH), dma(3, NCH), dma(7, NCH), dma(7, NCH),
+            dma(17), dma(96), dma(96), dma(3, NCH), dma(3, NCH), dma(7, NCH), dma(7, NCH),
             dma(7, NCH), dma(7, NCH), dma(3, NCH), dma(3, NCH),
             dma(2), dma(2), dma(2), dma(2),
         ],

time: 116 us -> 115 us (level)
  Pallas kernels: 115 us -> 113 us
    pallas_call x1, Pallas kernels: 113 us -> 111 us  [body(): pl.pallas_call(kernel, out_shape=outs, in_specs=[hbm] * 8, out_specs=(hbm...]
where the time goes in v4:
time: 115 us; the launch traced here: 113 us
  Pallas kernels  113 us (98%)
    pallas_call x1, Pallas kernels, body(): pl.pallas_call(kernel, out_shape=outs, in_specs=[hbm] * 8, out_specs=(hbm...  111 us

profile of v4, /device:TPU:6, one launch (start us, length us, event | category | flops | bytes accessed | tf_op | source)
XLA Modules:
  0.0 113.4 jit_solution(3282347867541976381)
XLA Ops:
  0.6 110.8 %shard_map.103 = (bf16[1,4096]{1,0:T(2,128)(2,1)}, f32[1,8]{1,0:T(1,128)}, bf16[96,4096]{1,0:T(8,128)(2,1)}) custom-call(bf16[1,4096]{1,0:T(2,128)(2,1)} %grad_in.1, bf16[1,8]{1,0:T(2,128)(2,1)} %weights_in.1, s32[1,8]{1,0:T(1,128)} %ids_in.1, s32[1,8]{1,0:T(1,128)} %places_in.1, bf16[1,192,240]{2,1,0:T(8,128)(2,1)} %bitcast.2, ...), custom_call_target="tpu_custom_call" | custom-call | tf_op jit(solution)/shard_map/pallas_call | solution.py:429
  111.5 1.9 %shard_map.104 = (bf16[1,4096]{1,0:T(2,128)(2,1)}, f32[1,8]{1,0:T(1,128)}, bf16[96,4096]{1,0:T(8,128)(2,1)}) custom-call(bf16[1,4096]{1,0:T(2,128)(2,1)} %get-tuple-element.9.tok, f32[1,8]{1,0:T(1,128)} %get-tuple-element.10.prob, bf16[96,4096]{1,0:T(8,128)(2,1)} %get-tuple-element.11.down), custom_call_target="tpu_custom_call" | custom-call | tf_op jit(solution)/shard_map/pallas_call | solution.py:479

commit v5 on v4

--- a/solution.py
+++ b/solution.py
@@ -15,9 +15,11 @@
 OWN, BOTH = 8, 16
 WO, WB = OWN * 128, BOTH * 128
 WIDE = EXT + WO + WB
-CUTS = [(0, EXT + WO // 2), (EXT + WO // 2, WO // 2), (EXT + WO, WB // 2), (EXT + WO + WB // 2, WB // 2)]
+FIRST = 2 * 128
+PARTS = [(0, FIRST), (FIRST, WO - FIRST)]
+CUTS = [(0, EXT + FIRST), (EXT + FIRST, WO - FIRST), (EXT + WO, WB // 2), (EXT + WO + WB // 2, WB // 2)]
 NCH = len(CUTS)
-BACK_ORDER = (2, 3, 0, 1)
+BACK_ORDER = (2, 3, 1, 0)
 
 
 def features(f):
@@ -212,7 +214,6 @@
     gate_factor = up_pre * sig * (1.0 + gate_pre * (1.0 - sig))
 
     pair = at_z(1 - 2 * odd)
-    half = WO // 2
     forwards = []
     back = jnp.zeros((ROWS, 128), F32)
     for f in range(NCH):
@@ -221,14 +222,14 @@
             copy.wait_recv()
         if f < 2:
             forwards.append(send(
-                yrecv.at[:, pl.ds(begin, half)], yrecv.at[:, pl.ds(WIDE + f * half, half)],
+                yrecv.at[:, pl.ds(begin, end - begin)], yrecv.at[:, pl.ds(WIDE + PARTS[f][0], end - begin)],
                 f_s.at[f], f_r.at[f], pair))
         back = back + dot(yrecv[:, begin:end], wdn[:, begin - EXT:end - EXT], ((1,), (1,)))
         sent += dispatch[f] + gathers[f]
     for f in range(2):
         forwards[f].wait_recv()
-        begin = WIDE + f * half
-        back = back + dot(yrecv[:, begin:begin + half], wdn[:, begin - EXT:begin - EXT + half], ((1,), (1,)))
+        begin, end = WIDE + PARTS[f][0], WIDE + sum(PARTS[f])
+        back = back + dot(yrecv[:, begin:end], wdn[:, begin - EXT:end - EXT], ((1,), (1,)))
     sent += forwards
 
     ext = yrecv[:, 0:EXT].astype(F32)
@@ -241,12 +242,13 @@
     psend[:, 0:EXT] = jnp.where(named, part_prob, 0.0).astype(BF)
     weighted = jnp.transpose(weight * product).astype(BF)
 
-    swaps = []
-    for f in range(2):
-        begin = WO + WB + f * half
-        zsend[:, f * half:(f + 1) * half] = dot(grads, wgu[:, begin:begin + half]).astype(BF)
-        part = pl.ds(f * half, half)
-        swaps.append(send(zsend.at[:, part], zrecv.at[:, part], z_s.at[f], z_r.at[f], pair))
+    swaps = {}
+    for f in (1, 0):
+        at, width = PARTS[f]
+        begin = WO + WB + at
+        zsend[:, at:at + width] = dot(grads, wgu[:, begin:begin + width]).astype(BF)
+        part = pl.ds(at, width)
+        swaps[f] = send(zsend.at[:, part], zrecv.at[:, part], z_s.at[f], z_r.at[f], pair)
     combine = [None] * NCH
     for f in BACK_ORDER:
         start, width = CUTS[f]
@@ -255,7 +257,7 @@
         part = dot(grads, wgu[:, begin - EXT:end - EXT])
         if f < 2:
             swaps[f].wait_recv()
-            part = part + zrecv[:, f * half:(f + 1) * half].astype(F32)
+            part = part + zrecv[:, PARTS[f][0]:sum(PARTS[f])].astype(F32)
         psend[:, begin:end] = part.astype(BF)
         copies = []
         for j, step in enumerate(EXP_STEPS):
@@ -268,7 +270,7 @@
         if f == 3:
             for at, begin, width in ((0, EXT + WO, WB), (own_at, EXT, WO), (other_at, WIDE, WO)):
                 gdown[:, pl.ds(at, width)] = dot(weighted, yrecv[:, begin:begin + width])[0:UNITS].astype(BF)
-    sent += swaps
+    sent += swaps.values()
     stores = [pltpu.make_async_copy(gdown, down_out, load_sem.at[5])]
     stores[0].start()
 
@@ -333,13 +335,13 @@
 
     combine_rows(2)
     combine_rows(3)
-    combine_rows(0)
+    combine_rows(1)
     sum_rows(2)
     sum_rows(3)
     near = {0: send_near(0)}
-    combine_rows(1)
+    combine_rows(0)
+    sum_rows(1)
     sum_rows(0)
-    sum_rows(1)
     near[1] = send_near(1)
 
     def send_far(h):

time: 115 us -> 114 us (level)
  no operation moved by 1% of the time
where the time goes in v5:
time: 114 us; the launch traced here: 113 us
  Pallas kernels  112 us (98%)
    pallas_call x1, Pallas kernels, body(): pl.pallas_call(kernel, out_shape=outs, in_specs=[hbm] * 8, out_specs=(hbm...  110 us

profile of v5, /device:TPU:6, one launch (start us, length us, event | category | flops | bytes accessed | tf_op | source)
XLA Modules:
  0.0 112.7 jit_solution(7906717189981011760)
XLA Ops:
  0.6 110.1 %shard_map.103 = (bf16[1,4096]{1,0:T(2,128)(2,1)}, f32[1,8]{1,0:T(1,128)}, bf16[96,4096]{1,0:T(8,128)(2,1)}) custom-call(bf16[1,4096]{1,0:T(2,128)(2,1)} %grad_in.1, bf16[1,8]{1,0:T(2,128)(2,1)} %weights_in.1, s32[1,8]{1,0:T(1,128)} %ids_in.1, s32[1,8]{1,0:T(1,128)} %places_in.1, bf16[1,192,240]{2,1,0:T(8,128)(2,1)} %bitcast.2, ...), custom_call_target="tpu_custom_call" | custom-call | tf_op jit(solution)/shard_map/pallas_call | solution.py:431
  110.8 1.9 %shard_map.104 = (bf16[1,4096]{1,0:T(2,128)(2,1)}, f32[1,8]{1,0:T(1,128)}, bf16[96,4096]{1,0:T(8,128)(2,1)}) custom-call(bf16[1,4096]{1,0:T(2,128)(2,1)} %get-tuple-element.9.tok, f32[1,8]{1,0:T(1,128)} %get-tuple-element.10.prob, bf16[96,4096]{1,0:T(8,128)(2,1)} %get-tuple-element.11.down), custom_call_target="tpu_custom_call" | custom-call | tf_op jit(solution)/shard_map/pallas_call | solution.py:481
